TPU v7x, 512 devices: a whole 4x4x16 slice. The times are simulated.
512 devices in a mesh: prow: 64 (over x, z), pcol: 8 (over y, core).
Axes of the slice: x: 4, y: 4, z: 16, core: 2. Of those that a mesh axis runs over, the one named last changes fastest.
Arguments:
- matrix: float32 [16384, 4096], P('prow', 'pcol'), may hold values from -6 to 6
- pivots: int32 [512], replicated, may hold values from 512 to 16383, as said below
- lower_inv: float32 [4, 128, 128], replicated, as said below
- upper_inv: float32 [4, 128, 128], replicated, as said below
Outputs:
- factored: float32 [16384, 4096], P('prow', 'pcol')
Inputs may be any that keep to these rules, and one draw needn't show every extreme that they name: The pivots are distinct and each names a row below the first 512 rows; both ends of the range occur in every draw. `lower_inv`: each block is lower triangular with a positive diagonal. `upper_inv`: each block is upper triangular with a positive diagonal.
All inputs are finite; a program needn't handle non-finite values.
Results may differ from a plain program's by a relative error of at most 0.00014.
Values sent between devices are 32-bit elements; how exact they have to be, the bound alone decides.
No kernel may reach another device: no remote copies, remote signals or barrier semaphores. Data moves between devices by JAX's collectives and lax.ppermute only.
A program may use at most 64 MiB of HBM per device.

v0:
```python
import jax
import jax.numpy as jnp
from jax import lax
from jax.sharding import PartitionSpec as P


def spread(array, axis, root):
    mine = lax.axis_index(axis) == root
    return lax.psum(jnp.where(mine, array, jnp.zeros_like(array)), axis)


def product(left, right):
    return jnp.dot(left, right, precision=lax.Precision.HIGHEST, preferred_element_type=jnp.float32)


def panel_step(block, inner_width, lower_inv, upper_inv, panel_rows, panel_top):
    begin_col = block * inner_width
    end_col = begin_col + inner_width
    upper_block = product(lower_inv[block], panel_top[begin_col:end_col])
    lower_rows = product(panel_rows[:, begin_col:end_col], upper_inv[block])
    lower_top = product(panel_top[:, begin_col:end_col], upper_inv[block])
    panel_rows = panel_rows.at[:, end_col:].add(-product(lower_rows, upper_block[:, end_col:]))
    panel_top = panel_top.at[:, end_col:].add(-product(lower_top, upper_block[:, end_col:]))
    return (upper_block, lower_rows, lower_top, panel_rows, panel_top)


def per_device(matrix, pivots, lower_inv, upper_inv):
    row_count, panel_width = matrix.shape
    blocks = lower_inv.shape[0]
    inner_width = lower_inv.shape[1]
    first_row = lax.axis_index("prow") * row_count
    owned_here = pivots // row_count == lax.axis_index("prow")
    pivot_local = pivots % row_count
    top_global = jnp.arange(panel_width, dtype=jnp.int32)
    top_here = (top_global >= first_row) & (top_global < first_row + row_count)
    top_local = jnp.clip(top_global - first_row, 0, row_count - 1)
    incoming = jnp.where(owned_here[:, None], matrix[pivot_local], jnp.float32(0.0))
    outgoing = jnp.where(top_here[:, None], matrix[top_local], jnp.float32(0.0))
    new_top, old_top = lax.psum((incoming, outgoing), "prow")
    swapped = matrix.at[jnp.where(owned_here, pivot_local, row_count)].set(old_top, mode="drop")
    swapped = swapped.at[jnp.where(top_here, top_global - first_row, row_count)].set(
        new_top, mode="drop"
    )
    remainder = new_top
    columns = jnp.arange(panel_width, dtype=jnp.int32)
    trailing = swapped
    panel_rows = swapped
    panel_top = new_top
    upper_blocks = []
    lower_parts = []
    urow_blocks = []
    top_parts = []
    for block in range(blocks):
        upper_block, lower_rows, lower_top, panel_rows, panel_top = panel_step(
            block, inner_width, lower_inv, upper_inv, panel_rows, panel_top
        )
        upper_blocks.append(
            jnp.where(columns[None, :] >= block * inner_width, upper_block, jnp.float32(0.0))
        )
        lower_parts.append(lower_rows)
        top_parts.append(lower_top)
    sent_rows, sent_top = (
        spread(jnp.concatenate(lower_parts, axis=1), "pcol", 0),
        spread(jnp.concatenate(top_parts, axis=1), "pcol", 0),
    )
    for block in range(blocks):
        begin_col = block * inner_width
        end_col = begin_col + inner_width
        next_remainder = remainder
        next_lower_top = sent_top[:, begin_col:end_col]
        next_begin_col = block * inner_width
        next_end_col = next_begin_col + inner_width
        urow_part = product(lower_inv[block], next_remainder[next_begin_col:next_end_col])
        next_remainder = next_remainder.at[next_end_col:].add(
            -product(next_lower_top[next_end_col:], urow_part)
        )
        remainder = next_remainder
        urow_blocks.append(urow_part)
        trailing = trailing - product(sent_rows[:, begin_col:end_col], urow_part)
    panel_upper = jnp.concatenate(upper_blocks, axis=0)
    urow_all = jnp.concatenate(urow_blocks, axis=0)
    lower_all = jnp.concatenate(lower_parts, axis=1)
    row_global = first_row + jnp.arange(row_count, dtype=jnp.int32)
    top_mask = row_global < panel_width
    top_pick = jnp.clip(row_global, 0, panel_width - 1)
    panel_out = jnp.where(top_mask[:, None], panel_upper[top_pick], lower_all)
    trailing_out = jnp.where(top_mask[:, None], urow_all[top_pick], trailing)
    return jnp.where(lax.axis_index("pcol") == 0, panel_out, trailing_out)


def solution(mesh):
    in_specs = (P("prow", "pcol"), P(), P(), P())
    out_specs = P("prow", "pcol")
    return jax.shard_map(
        per_device, mesh=mesh, in_specs=in_specs, out_specs=out_specs, check_vma=False
    )
```

profile of v0, /device:TPU:1, one launch (start us, length us, event | category | flops | bytes accessed | tf_op | source)
XLA Modules:
  0.0 423.3 jit_solution(13851341678697139162)
XLA Ops:
  6.5 1.0 copy.59
  8.3 1.6 gather_fusion
  10.3 2.3 gather_fusion.2
  12.6 1.6 copy.27
  14.2 1.5 broadcast_select_fusion
  15.8 274.2 %all-reduce.5.cloned.1.call-done = (f32[512,512]{0,1:T(8,128)}, f32[512,512]{0,1:T(8,128)}) async-done(((f32[512,512]{0,1:T(8,128)}, f32[512,512]{0,1:T(8,128)}), (f32[512,512]{0,1:T(8,128)}, f32[512,512]{0,1:T(8,128)})) %all-reduce.5.cloned.1.call-update) | async-done | bytes 2097168 | tf_op jit(solution)/shard_map/psum | solution.py:39
  290.1 2.6 copy.29
  292.7 1.0 copy.51
  294.3 1.3 copy.28
  295.6 1.3 fusion.30
  297.3 0.8 fusion.1
  298.6 3.1 scatter_fusion
  301.7 3.3 scatter_fusion.1
  306.7 0.9 constant_dynamic-update-slice_fusion.2
  307.6 2.0 broadcast_select_fusion.3
  309.7 1.4 constant_dynamic-update-slice_fusion.1
  312.3 2.0 broadcast_select_fusion.2
  314.3 1.1 constant_dynamic-update-slice_fusion
  316.6 1.1 maximum_select_fusion
  317.7 0.8 fusion.16
  319.5 2.1 fusion.7
  321.6 79.3 %all-reduce.7.cloned.1.call-done = (f32[512,512]{0,1:T(8,128)}, f32[256,512]{0,1:T(8,128)}) async-done(((f32[512,512]{0,1:T(8,128)}, f32[256,512]{0,1:T(8,128)}), (f32[512,512]{0,1:T(8,128)}, f32[256,512]{0,1:T(8,128)})) %all-reduce.7.cloned.1.call-update) | async-done | bytes 1572880 | tf_op jit(solution)/shard_map/psum | solution.py:9
  400.9 1.8 fusion
  403.1 1.6 fusion.3
  406.4 1.4 fusion.8
  407.8 1.2 fusion.53
  409.1 1.4 convolution_subtract_fusion.1
  410.7 1.0 gather_fusion.1
  411.7 1.0 gather_fusion.3
  413.1 0.8 copy-done.1
  413.9 1.5 fusion.5
  415.5 1.0 copy.39
  (63 shorter events, 10.1 us)
Async XLA Ops:
  6.5 283.5 %all-reduce.5.cloned.1.call-start = ((), (), s32[]{:S(2)}) async-start(), calls=%async_computation | async-start | bytes 4194304 | tf_op jit(solution)/shard_map/psum | solution.py:39
  7.6 0.7 copy-start.13
  15.7 385.2 %all-reduce.7.cloned.1.call-start = ((), (), s32[]{:S(2)}) async-start(), calls=%async_computation.1 | async-start | bytes 3145728 | tf_op jit(solution)/shard_map/psum | solution.py:9
  290.1 2.6 copy-start
  292.7 1.6 copy-start.6
  295.6 1.3 copy-start.4
  305.4 1.0 copy-start.5
  306.7 1.0 copy-start.10
  316.2 1.5 copy-start.2
  318.6 1.0 copy-start.11
  403.1 1.6 copy-start.12
  409.0 1.4 copy-start.7
  409.1 1.4 copy-start.8
  409.1 1.4 copy-start.9
  412.9 1.0 copy-start.1
  412.9 1.1 copy-start.3
Sparse Core Ops, SparseCore 0:
  15.9 274.1 all-reduce.4
  318.6 82.2 all-reduce.6
where the time goes:
time: 425 us; the launch traced here: 423 us
  waiting for transfers between devices  354 us (83%)
  local copies, waits for them, and re-layouts  26 us (6%)
  matrix products  26 us (6%)
  between operations  13.8 us (3%)
    psum x1, waiting for transfers between devices, per_device(): new_top, old_top = lax.psum((incoming, outgoing), 'prow')  274 us
    psum x1, waiting for transfers between devices, spread(): return lax.psum(jnp.where(mine, array, jnp.zeros_like(array)), axis)  79.3 us
    dot_general x28, matrix products, product(): jnp.dot(left, right, precision=lax.Precision.HIGHEST, preferred_element_t...  26 us
  transfers between devices with their start and end apart: 2, of which 2 were waited for; matrix products, arithmetic and copies ran while one was open for 1% of the time, Pallas kernels for 0%

commit v1 on v0

v1 whole, which is shorter than its diff:
```python
import functools

import jax
import jax.numpy as jnp
from jax import lax
from jax.experimental import pallas as pl
from jax.experimental.pallas import tpu as pltpu
from jax.sharding import PartitionSpec as P

ROWS = 256
NB = 512
IB = 128
BLOCKS = NB // IB
XN = 4
ZN = 16
CAP_OWN = 24
CAP_X = 176
CAP_ZB = 96
CAP_Z = 40

VMEM = pl.BlockSpec(memory_space=pltpu.VMEM)
SMEM = pl.BlockSpec(memory_space=pltpu.SMEM)
PARAMS = pltpu.CompilerParams(vmem_limit_bytes=48 * 1024 * 1024)
F32 = jnp.float32
BF16 = jnp.bfloat16


def product(left, right):
    return jnp.dot(left, right, precision=lax.Precision.HIGHEST, preferred_element_type=F32)


def exact_parts(values):
    high = values.astype(BF16)
    rest = values - high.astype(F32)
    middle = rest.astype(BF16)
    low = (rest - middle.astype(F32)).astype(BF16)
    return high, middle, low


def pick(chosen, values):
    high, middle, low = exact_parts(values)
    small = jnp.dot(chosen, middle, preferred_element_type=F32) + jnp.dot(
        chosen, low, preferred_element_type=F32
    )
    return jnp.dot(chosen, high, preferred_element_type=F32) + small


def ones_at(condition):
    return jnp.where(condition, F32(1.0), F32(0.0)).astype(BF16)


def match(slots, key, mask=None):
    rows = lax.broadcasted_iota(jnp.int32, (slots, key.shape[1]), 0)
    if mask is not None:
        key = jnp.where(mask, key, -1)
    return ones_at(rows == key)


def joined(target, source):
    both = lax.dot_general(target, source, (((1,), (1,)), ((), ())), preferred_element_type=F32)
    return both.astype(BF16)


def unpack(pivots):
    owner = pivots >> 8
    index = lax.broadcasted_iota(jnp.int32, pivots.shape, 1)
    return owner, pivots & 255, owner >> 4, owner & 15, index >> 8


def prep_kernel(place, piv_ref, mat_ref, ranks_ref, cols_ref, asend_ref, dmsg_ref, ok_ref):
    row = place[0]
    pivots = piv_ref[...]
    owner, local, x_of, z_of, half = unpack(pivots)
    classes = jnp.concatenate(
        [
            match(64, owner),
            match(16, x_of),
            match(16, half * 4 + (z_of >> 2)),
            match(32, half * 16 + z_of),
        ],
        axis=0,
    )
    before = ones_at(
        lax.broadcasted_iota(jnp.int32, (NB, NB), 0) < lax.broadcasted_iota(jnp.int32, (NB, NB), 1)
    )
    counts = jnp.dot(classes, before, preferred_element_type=F32) * classes.astype(F32)
    own = jnp.sum(counts[:64], axis=0, keepdims=True)
    in_x = jnp.sum(counts[64:80], axis=0, keepdims=True)
    in_zb = jnp.sum(counts[80:96], axis=0, keepdims=True)
    in_z = jnp.sum(counts[96:128], axis=0, keepdims=True)
    fits = (
        (jnp.max(own) < CAP_OWN)
        & (jnp.max(in_x) < CAP_X)
        & (jnp.max(in_zb) < CAP_ZB)
        & (jnp.max(in_z) < CAP_Z)
    )
    ok_ref[0] = jnp.where(fits, 1, 0).astype(jnp.int32)
    zero = jnp.zeros_like(own)
    ranks = jnp.concatenate([own, in_x, in_zb, in_z, zero, zero, zero, zero], axis=0)
    ranks_ref[...] = ranks.astype(jnp.int32)
    wanted = jnp.concatenate(
        [x_of.astype(F32), jnp.minimum(in_x, 255.0), zero, zero, zero, zero, zero, zero], axis=0
    ).astype(BF16)
    diagonal = ones_at(
        lax.broadcasted_iota(jnp.int32, (NB, NB), 0) == lax.broadcasted_iota(jnp.int32, (NB, NB), 1)
    )
    cols_ref[...] = lax.dot_general(
        diagonal, wanted, (((1,), (1,)), ((), ())), preferred_element_type=F32
    ).astype(jnp.int32)
    own_rank = own.astype(jnp.int32)
    chosen = joined(match(CAP_OWN, own_rank, owner == row), match(ROWS, local))
    asend_ref[...] = pick(chosen, mat_ref[...])

    @pl.when(row < 2)
    def _():
        rank = in_zb.astype(jnp.int32)
        block = z_of >> 2
        rank = jnp.where(row == 0, rank[:, :ROWS], rank[:, ROWS:])
        block = jnp.where(row == 0, block[:, :ROWS], block[:, ROWS:])
        chosen = jnp.concatenate([match(CAP_ZB, rank, block == a) for a in range(4)], axis=0)
        dmsg_ref[...] = pick(chosen, mat_ref[...])


def group_kernel(place, piv_ref, ranks_ref, gathered_ref, amsg_ref):
    row = place[0]
    owner, local, x_of, z_of, half = unpack(piv_ref[...])
    ranks = ranks_ref[...]
    target = match(CAP_X, ranks[1:2], x_of == (row >> 4))
    source = match(ZN * CAP_OWN, z_of * CAP_OWN + ranks[0:1])
    amsg_ref[...] = pick(joined(target, source), gathered_ref[...])


def near_kernel(place, piv_ref, ranks_ref, dmsg_ref, r1_ref, r2_ref, r3_ref, m0, m1, m2, m3):
    row = place[0]

    @pl.when((row < ZN) & ((row & 3) < 2))
    def _():
        owner, local, x_of, z_of, half = unpack(piv_ref[...])
        ranks = ranks_ref[...]
        side = row & 1
        rows = jnp.where(row < 2, dmsg_ref[:CAP_ZB], r1_ref[...] + r2_ref[...] + r3_ref[...])
        source = match(CAP_ZB, ranks[2:3])
        for out, to in zip((m0, m1, m2, m3), (side, 1 - side, 2 + side, 3 - side)):
            plane = (row & 12) + to
            target = match(CAP_Z, ranks[3:4], (half == side) & (z_of == plane))
            out[...] = pick(joined(target, source), rows)


def spread_kernel(place, piv_ref, ranks_ref, m0, r1, r2, r3, d0, d1, d2, d3):
    row = place[0]

    @pl.when(row < ZN)
    def _():
        owner, local, x_of, z_of, half = unpack(piv_ref[...])
        ranks = ranks_ref[...]
        spot = row & 3
        first = jnp.where(spot < 2, m0[...], r2[...])
        second = jnp.where(spot < 2, r1[...], r3[...])
        rows = jnp.concatenate([first, second], axis=0)
        slot = ranks[3:4] + jnp.where(half == (spot & 1), 0, CAP_Z)
        source = match(2 * CAP_Z, slot)
        for x, out in enumerate((d0, d1, d2, d3)):
            target = match(CAP_OWN, ranks[0:1], owner == row + x * ZN)
            out[...] = pick(joined(target, source), rows)


def factor(place, top_ref, linv_ref, uinv_ref, w_ref, v_ref, upper_ref):
    row = place[0]
    w_ref[...] = jnp.zeros((NB, NB), F32)
    v_ref[...] = jnp.zeros((NB, NB), F32)
    upper_ref[...] = jnp.zeros((ROWS, NB), F32)
    eye = jnp.where(
        lax.broadcasted_iota(jnp.int32, (IB, IB), 0) == lax.broadcasted_iota(jnp.int32, (IB, IB), 1),
        F32(1.0),
        F32(0.0),
    )
    for block in range(BLOCKS):
        begin, end = block * IB, (block + 1) * IB
        linv, uinv = linv_ref[block], uinv_ref[block]
        upper = product(linv, top_ref[begin:end, begin:])

        @pl.when(row == begin // ROWS)
        def _():
            upper_ref[begin % ROWS : begin % ROWS + IB, begin:] = upper

        if begin:
            v_left = product(linv, v_ref[begin:end, :begin])
            v_ref[begin:end, :begin] = v_left
            w_up = product(w_ref[:begin, begin:end], uinv)
            w_ref[:begin, begin:end] = w_up
        v_ref[begin:end, begin:end] = linv
        w_ref[begin:end, begin:end] = uinv
        if end < NB:
            lower = product(top_ref[end:, begin:end], uinv)
            top_ref[end:, end:] -= product(lower, upper[:, IB:])
            v_ref[end:, :end] -= product(lower, v_ref[begin:end, :end])
            w_ref[:end, end:] -= product(w_ref[:end, begin:end], upper[:, IB:])


def order_kernel(place, cols_ref, a0, a1, a2, a3, linv, uinv, top_ref, w_ref, v_ref, upper_ref, work):
    row, col = place[0], place[1]
    cols = cols_ref[...]
    slot = (((row >> 4) - cols[:, 0:1]) & 3) * CAP_X + cols[:, 1:2]
    chosen = ones_at(lax.broadcasted_iota(jnp.int32, (NB, XN * CAP_X), 1) == slot)
    rows = jnp.concatenate([a0[...], a1[...], a2[...], a3[...]], axis=0)
    top = pick(chosen, rows)
    top_ref[...] = top

    @pl.when(col == 0)
    def _():
        work[...] = top
        factor(place, work, linv, uinv, w_ref, v_ref, upper_ref)


def factor_kernel(place, top_ref, linv, uinv, w_ref, v_ref, upper_ref, work):
    @pl.when(place[1] == 0)
    def _():
        work[...] = top_ref[...]
        factor(place, work, linv, uinv, w_ref, v_ref, upper_ref)


def placed(row, piv_ref, ranks_ref, mat_ref, d0, d1, d2, d3):
    owner, local, x_of, z_of, half = unpack(piv_ref[...])
    rows = jnp.where(row < ZN, d0[...], d1[...] + d2[...] + d3[...])
    mine = owner == row
    target = match(ROWS, local, mine)
    source = match(CAP_OWN, ranks_ref[0:1], mine)
    chosen = joined(target, source)
    hit = jnp.sum(chosen.astype(F32), axis=1, keepdims=True) > 0.5
    return jnp.where(hit, pick(chosen, rows), mat_ref[...])


def rows_kernel(moved, place, *refs):
    if moved:
        piv_ref, ranks_ref, mat_ref, d0, d1, d2, d3, w_ref, v_ref, upper_ref, q_ref, out_ref = refs
    else:
        mat_ref, w_ref, v_ref, upper_ref, q_ref, out_ref = refs
    row, col = place[0], place[1]

    @pl.when((col == 0) & (row < 2))
    def _():
        q_ref[...] = -jnp.where(row == 0, v_ref[:ROWS], v_ref[ROWS:])
        out_ref[...] = upper_ref[...]

    @pl.when((col == 0) & (row >= 2))
    def _():
        if moved:
            rows = placed(row, piv_ref, ranks_ref, mat_ref, d0, d1, d2, d3)
        else:
            rows = mat_ref[...]
        lower = product(rows, w_ref[...])
        out_ref[...] = lower
        q_ref[...] = product(lower, v_ref[...])


def final_kernel(moved, place, *refs):
    if moved:
        piv_ref, ranks_ref, mat_ref, d0, d1, d2, d3, q_ref, top_ref, panel_ref, out_ref = refs
    else:
        mat_ref, q_ref, top_ref, panel_ref, out_ref = refs
    row, col = place[0], place[1]

    @pl.when(col == 0)
    def _():
        out_ref[...] = panel_ref[...]

    @pl.when(col != 0)
    def _():
        change = product(q_ref[...], top_ref[...])
        if moved:
            rows = placed(row, piv_ref, ranks_ref, mat_ref, d0, d1, d2, d3)
        else:
            rows = mat_ref[...]
        out_ref[...] = jnp.where(row < 2, F32(0.0), rows) - change


def shape(rows, cols=NB, dtype=F32):
    return jax.ShapeDtypeStruct((rows, cols), dtype)


def call(kernel, out_shape, *args, scratch=(), out_specs=None):
    if out_specs is None:
        out_specs = jax.tree.map(lambda _: VMEM, out_shape)
    return pl.pallas_call(
        kernel,
        out_shape=out_shape,
        in_specs=[SMEM] + [VMEM] * (len(args) - 1),
        out_specs=out_specs,
        scratch_shapes=list(scratch),
        compiler_params=PARAMS,
    )(*args)


def shift_x(array, by):
    return lax.ppermute(array, "prow", [(i, (i + by * ZN) % (XN * ZN)) for i in range(XN * ZN)])


def broadcast(q):
    col = lax.axis_index("pcol")
    parts = [lax.ppermute(q, "pcol", [(0, to)]) for to in (4, 2, 6)]
    even = jnp.where(col == 0, q, parts[0] + parts[1] + parts[2])
    odd = lax.ppermute(even, "pcol", [(0, 1), (2, 3), (4, 5), (6, 7)])
    return jnp.where(col % 2 == 0, even, odd)


Z_RINGS = [[x * ZN + z for z in range(ZN)] for x in range(XN)]
PAIRS = [(4 * a, 4 * a + 1) for a in range(4)]
NEAR = [
    [(i, j) for i, j in PAIRS] + [(j, i) for i, j in PAIRS],
    [(i, i + 2) for i, j in PAIRS] + [(j, j + 2) for i, j in PAIRS],
    [(i, i + 3) for i, j in PAIRS] + [(j, j + 1) for i, j in PAIRS],
]


def direct(place, matrix, pivots, lower_inv, upper_inv, ranks, cols, asend, dmsg):
    far = [
        lax.ppermute(dmsg[a * CAP_ZB : (a + 1) * CAP_ZB], "prow", [(0, 4 * a), (1, 4 * a + 1)])
        for a in (1, 2, 3)
    ]
    gathered = lax.all_gather(asend, "prow", axis_index_groups=Z_RINGS, tiled=True)
    mine = call(group_kernel, shape(CAP_X), place, pivots, ranks, gathered)
    others = [shift_x(mine, by) for by in (1, 2, 3)]
    messages = call(near_kernel, [shape(CAP_Z)] * 4, place, pivots, ranks, dmsg, *far)
    near = [lax.ppermute(m, "prow", pairs) for m, pairs in zip(messages[1:], NEAR)]
    spread = call(spread_kernel, [shape(CAP_OWN)] * 4, place, pivots, ranks, messages[0], *near)
    moved = [spread[0]] + [
        lax.ppermute(spread[x], "prow", [(z, x * ZN + z) for z in range(ZN)]) for x in (1, 2, 3)
    ]
    top, w, v, upper = call(
        order_kernel,
        [shape(NB), shape(NB), shape(NB), shape(ROWS)],
        place, cols, mine, *others, lower_inv, upper_inv,
        scratch=[pltpu.VMEM((NB, NB), F32)],
    )
    q, panel = call(
        functools.partial(rows_kernel, True), [shape(ROWS)] * 2,
        place, pivots, ranks, matrix, *moved, w, v, upper,
    )
    q = broadcast(q)
    return call(
        functools.partial(final_kernel, True), shape(ROWS),
        place, pivots, ranks, matrix, *moved, q, top, panel,
    )


def general(place, matrix, pivots, lower_inv, upper_inv, ranks, cols, asend, dmsg):
    row = place[0]
    pivots = pivots[0]
    here = (pivots >> 8) == row
    local = pivots & 255
    index = jnp.arange(NB, dtype=jnp.int32)
    top_here = (index >> 8) == row
    both = jnp.concatenate(
        [
            jnp.where(here[:, None], matrix[local], F32(0.0)),
            jnp.where(top_here[:, None], matrix[index & 255], F32(0.0)),
        ],
        axis=0,
    )
    for bit in (1, 2, 4, 8, 16, 32):
        both = both + lax.ppermute(both, "prow", [(i, i ^ bit) for i in range(XN * ZN)])
    top, old = both[:NB], both[NB:]
    swapped = matrix.at[jnp.where(here, local, ROWS)].set(old, mode="drop")
    w, v, upper = call(
        factor_kernel, [shape(NB), shape(NB), shape(ROWS)],
        place, top, lower_inv, upper_inv,
        scratch=[pltpu.VMEM((NB, NB), F32)],
    )
    q, panel = call(
        functools.partial(rows_kernel, False), [shape(ROWS)] * 2, place, swapped, w, v, upper
    )
    q = broadcast(q)
    return call(functools.partial(final_kernel, False), shape(ROWS), place, swapped, q, top, panel)


def per_device(matrix, pivots, lower_inv, upper_inv):
    place = jnp.stack([lax.axis_index("prow"), lax.axis_index("pcol")]).astype(jnp.int32)
    pivots = pivots.reshape(1, NB)
    ranks, cols, asend, dmsg, fits = call(
        prep_kernel,
        [
            shape(8, NB, jnp.int32), shape(NB, 8, jnp.int32), shape(CAP_OWN), shape(4 * CAP_ZB),
            jax.ShapeDtypeStruct((1,), jnp.int32),
        ],
        place, pivots, matrix,
        out_specs=[VMEM, VMEM, VMEM, VMEM, SMEM],
    )
    return lax.cond(
        fits[0] == 1, direct, general,
        place, matrix, pivots, lower_inv, upper_inv, ranks, cols, asend, dmsg,
    )


def solution(mesh):
    in_specs = (P("prow", "pcol"), P(), P(), P())
    out_specs = P("prow", "pcol")
    return jax.shard_map(
        per_device, mesh=mesh, in_specs=in_specs, out_specs=out_specs, check_vma=False
    )
```

time: 425 us -> 125 us (0.29)
  the two profiles are of different devices: /device:TPU:1 before, /device:TPU:105 now
where the time goes in v1:
time: 125 us; the launch traced here: 124 us
  blocking collectives  46.6 us (37%)
  waiting for transfers between devices  38.8 us (31%)
  starting transfers between devices  22.6 us (18%)
  Pallas kernels  10.7 us (9%)
  local copies, waits for them, and re-layouts  2.68 us (2%)
  other arithmetic  1.73 us (1%)
    all_gather x1, blocking collectives, direct(): lax.all_gather(asend, 'prow', axis_index_groups=Z_RINGS, tiled=True)  46.6 us
    ppermute x1, waiting for transfers between devices, broadcast(): odd = lax.ppermute(even, 'pcol', [(0, 1), (2, 3), (4, 5), (6, 7)])  29.4 us
    pallas_call x7, Pallas kernels, call(): pl.pallas_call(kernel, out_shape=out_shape, in_specs=[SMEM] + [VMEM] * (l...  10.7 us
    ppermute x3, waiting for transfers between devices, direct(): lax.ppermute(m, 'prow', pairs)  9.37 us
    ppermute x3, starting transfers between devices, shift_x(): lax.ppermute(array, 'prow', [(i, (i + by * ZN) % (XN * ZN)) for i in rang...  8.41 us
    ppermute x3, starting transfers between devices, direct(): lax.ppermute(spread[x], 'prow', [(z, x * ZN + z) for z in range(ZN)])  3.88 us
    ppermute x3, starting transfers between devices, broadcast(): parts = [lax.ppermute(q, 'pcol', [(0, to)]) for to in (4, 2, 6)]  3.65 us
    ppermute x3, starting transfers between devices, direct(): lax.ppermute(m, 'prow', pairs)  3.25 us
  transfers between devices with their start and end apart: 16, of which 3 were waited for; matrix products, arithmetic and copies ran while one was open for 0% of the time, Pallas kernels for 4%

profile of v1, /device:TPU:105, one launch (start us, length us, event | category | flops | bytes accessed | tf_op | source)
XLA Modules:
  0.0 124.4 jit_solution(9495829479831279911)
XLA Ops:
  0.0 1.0 copy.11.mat_ref
  1.1 2.3 %shard_map.48 = (s32[8,512]{1,0:T(8,128)S(1)}, s32[512,8]{1,0:T(8,128)}, f32[24,512]{1,0:T(8,128)S(1)}, f32[384,512]{1,0:T(8,128)S(1)}, s32[1]{0:T(128)}) custom-call(s32[2]{0:T(128)S(1)} %pad_add_fusion.place, s32[1,512]{1,0:T(1,128)} %bitcast.5, f32[256,512]{1,0:T(8,128)S(1)} %copy.11.mat_ref), custom_call_target="tpu_custom_call" | custom-call | tf_op jit(solution)/shard_map/pallas_call | solution.py:284
  4.1 119.5 %conditional.1 = (f32[256,512]{1,0:T(8,128)S(1)}) conditional(s32[]{:T(128)} %bitcast.4, (s32[512]{0:T(512)}, s32[]{:T(128)}, f32[256,512]{1,0:T(8,128)S(1)}, s32[2]{0:T(128)S(1)}, f32[4,128,128]{2,1,0:T(8,128)}, /*index=5*/f32[4,128,128]{2,1,0:T(8,128)}) %tuple.11, (f32[384,512]{1,0:T(8,128)S(1)}, s32[2]{0:T(128)S(1)}, s32[1,512]{1,0:T(1,128)}, ...), branch_computations={%region_0.2_spmd, %region_2.3_spmd} | conditional | flops 5254159 | bytes 129528480 | solution.py:388
  4.4 0.8 collective-permute-start.10
  5.2 0.7 collective-permute-start.11
  5.9 0.7 collective-permute-start.12
  6.6 46.6 %all_gather.2.gathered_ref = f32[384,512]{1,0:T(8,128)S(1)} all-gather(f32[24,512]{1,0:T(8,128)S(1)} %get-tuple-element.63), channel_id=1, replica_groups={{0,8,16,24,32,40,48,56,64,72,80,88,96,104,112,120},{128,136,144,152,160..., dimensions={0}, use_global_device_ids=true | all-gather | bytes 835584 | tf_op jit(solution)/shard_map/cond/branch_1_fun/all_gather | solution.py:320
  53.2 1.4 %branch_1_fun.8.a0 = f32[176,512]{1,0:T(8,128)S(1)} custom-call(s32[2]{0:T(128)S(1)} %get-tuple-element.49.place, s32[1,512]{1,0:T(1,128)} %get-tuple-element.50.piv_ref.refs_0_, s32[8,512]{1,0:T(8,128)S(1)} %get-tuple-element.51.ranks_ref.refs_1_, f32[384,512]{1,0:T(8,128)S(1)} %all_gather.2.gathered_ref), custom_call_target="tpu_custom_call" | custom-call | tf_op jit(solution)/shard_map/cond/branch_1_fun/pallas_call | solution.py:284
  54.6 1.9 %collective-permute-start.19 = (f32[176,512]{1,0:T(8,128)S(1)}, f32[176,512]{1,0:T(8,128)S(1)}, u32[]{:S(2)}, u32[]{:S(2)}) collective-permute-start(f32[176,512]{1,0:T(8,128)S(1)} %branch_1_fun.8.a0), channel_id=1, source_target_pairs={{0,128},{8,136},{16,144},{24,152},{32,160},{40,168},{48,176},{56,1... | collective-permute-start | bytes 1081352 | tf_op jit(solution)/shard_map/cond/branch_1_fun/ppermute | solution.py:295
  56.5 1.9 %collective-permute-start.20 = (f32[176,512]{1,0:T(8,128)S(1)}, f32[176,512]{1,0:T(8,128)S(1)}, u32[]{:S(2)}, u32[]{:S(2)}) collective-permute-start(f32[176,512]{1,0:T(8,128)S(1)} %branch_1_fun.8.a0), channel_id=1, source_target_pairs={{0,256},{8,264},{16,272},{24,280},{32,288},{40,296},{48,304},{56,3... | collective-permute-start | bytes 1081352 | tf_op jit(solution)/shard_map/cond/branch_1_fun/ppermute | solution.py:295
  58.5 4.6 %collective-permute-start.21 = (f32[176,512]{1,0:T(8,128)S(1)}, f32[176,512]{1,0:T(8,128)S(1)}, u32[]{:S(2)}, u32[]{:S(2)}) collective-permute-start(f32[176,512]{1,0:T(8,128)S(1)} %branch_1_fun.8.a0), channel_id=1, source_target_pairs={{0,384},{8,392},{16,400},{24,408},{32,416},{40,424},{48,432},{56,4... | collective-permute-start | bytes 1081352 | tf_op jit(solution)/shard_map/cond/branch_1_fun/ppermute | solution.py:295
  63.1 0.6 branch_1_fun.6
  63.7 0.7 collective-permute-start.13
  64.3 1.3 %collective-permute-start.14 = (f32[40,512]{1,0:T(8,128)S(1)}, f32[40,512]{1,0:T(8,128)S(1)}, u32[]{:S(2)}, u32[]{:S(2)}) collective-permute-start(f32[40,512]{1,0:T(8,128)S(1)} %get-tuple-element.56), channel_id=1, source_target_pairs={{0,16},{32,48},{64,80},{96,112},{8,24},{40,56},{72,88},{104,120},{... | collective-permute-start | bytes 245768 | tf_op jit(solution)/shard_map/cond/branch_1_fun/ppermute | solution.py:324
  65.6 1.3 %collective-permute-start.15 = (f32[40,512]{1,0:T(8,128)S(1)}, f32[40,512]{1,0:T(8,128)S(1)}, u32[]{:S(2)}, u32[]{:S(2)}) collective-permute-start(f32[40,512]{1,0:T(8,128)S(1)} %get-tuple-element.57), channel_id=1, source_target_pairs={{0,24},{32,56},{64,88},{96,120},{8,16},{40,48},{72,80},{104,112},{... | collective-permute-start | bytes 245768 | tf_op jit(solution)/shard_map/cond/branch_1_fun/ppermute | solution.py:324
  66.9 7.0 %collective-permute-done.14.r2 = f32[40,512]{1,0:T(8,128)S(1)} collective-permute-done((f32[40,512]{1,0:T(8,128)S(1)}, f32[40,512]{1,0:T(8,128)S(1)}, u32[]{:S(2)}, u32[]{:S(2)}) %collective-permute-start.14) | collective-permute-done | bytes 81952 | tf_op jit(solution)/shard_map/cond/branch_1_fun/ppermute | solution.py:324
  73.9 2.4 %collective-permute-done.15.r3 = f32[40,512]{1,0:T(8,128)S(1)} collective-permute-done((f32[40,512]{1,0:T(8,128)S(1)}, f32[40,512]{1,0:T(8,128)S(1)}, u32[]{:S(2)}, u32[]{:S(2)}) %collective-permute-start.15) | collective-permute-done | bytes 81952 | tf_op jit(solution)/shard_map/cond/branch_1_fun/ppermute | solution.py:324
  76.3 1.3 %branch_1_fun.7 = (f32[24,512]{1,0:T(8,128)S(1)}, f32[24,512]{1,0:T(8,128)S(1)}, f32[24,512]{1,0:T(8,128)S(1)}, f32[24,512]{1,0:T(8,128)S(1)}) custom-call(s32[2]{0:T(128)S(1)} %get-tuple-element.49.place, s32[1,512]{1,0:T(1,128)S(1)} %copy-done.9, s32[8,512]{1,0:T(8,128)S(1)} %get-tuple-element.51.ranks_ref.refs_1_, f32[40,512]{1,0:T(8,128)S(1)} %get-tuple-element.54.m0, ...), custom_call_target="tpu_custom_call" | custom-call | tf_op jit(solution)/shard_map/cond/branch_1_fun/pallas_call | solution.py:284
  77.6 1.3 %collective-permute-start.16 = (f32[24,512]{1,0:T(8,128)S(1)}, f32[24,512]{1,0:T(8,128)S(1)}, u32[]{:S(2)}, u32[]{:S(2)}) collective-permute-start(f32[24,512]{1,0:T(8,128)S(1)} %get-tuple-element.59), channel_id=1, source_target_pairs={{0,128},{8,136},{16,144},{24,152},{32,160},{40,168},{48,176},{56,1... | collective-permute-start | bytes 147464 | tf_op jit(solution)/shard_map/cond/branch_1_fun/ppermute | solution.py:327
  78.9 1.3 %collective-permute-start.17 = (f32[24,512]{1,0:T(8,128)S(1)}, f32[24,512]{1,0:T(8,128)S(1)}, u32[]{:S(2)}, u32[]{:S(2)}) collective-permute-start(f32[24,512]{1,0:T(8,128)S(1)} %get-tuple-element.60), channel_id=1, source_target_pairs={{0,256},{8,264},{16,272},{24,280},{32,288},{40,296},{48,304},{56,3... | collective-permute-start | bytes 147464 | tf_op jit(solution)/shard_map/cond/branch_1_fun/ppermute | solution.py:327
  80.2 1.3 %collective-permute-start.18 = (f32[24,512]{1,0:T(8,128)S(1)}, f32[24,512]{1,0:T(8,128)S(1)}, u32[]{:S(2)}, u32[]{:S(2)}) collective-permute-start(f32[24,512]{1,0:T(8,128)S(1)} %get-tuple-element.61), channel_id=1, source_target_pairs={{0,384},{8,392},{16,400},{24,408},{32,416},{40,424},{48,432},{56,4... | collective-permute-start | bytes 147464 | tf_op jit(solution)/shard_map/cond/branch_1_fun/ppermute | solution.py:327
  81.6 2.2 %branch_1_fun.9 = (f32[512,512]{1,0:T(8,128)S(1)}, f32[512,512]{1,0:T(8,128)S(1)}, f32[512,512]{1,0:T(8,128)S(1)}, f32[256,512]{1,0:T(8,128)S(1)}) custom-call(s32[2]{0:T(128)S(1)} %get-tuple-element.49.place, s32[512,8]{1,0:T(8,128)S(1)} %copy-done.8, f32[176,512]{1,0:T(8,128)S(1)} %branch_1_fun.8.a0, f32[176,512]{1,0:T(8,128)S(1)} %collective-permute-done.19.a1, ...), custom_call_target="tpu_custom_call" | custom-call | tf_op jit(solution)/shard_map/cond/branch_1_fun/pallas_call | solution.py:284
  83.8 0.6 branch_1_fun.10
  84.4 0.7 collective-permute-start.24
  85.1 1.5 %collective-permute-start.22 = (f32[256,512]{1,0:T(8,128)S(1)}, f32[256,512]{1,0:T(8,128)}, u32[]{:S(2)}, u32[]{:S(2)}) collective-permute-start(f32[256,512]{1,0:T(8,128)S(1)} %get-tuple-element.69), channel_id=1, source_target_pairs={{0,4},{8,12},{16,20},{24,28},{32,36},{40,44},{48,52},{56,60},{64,6... | collective-permute-start | bytes 1572872 | tf_op jit(solution)/shard_map/cond/branch_1_fun/ppermute | solution.py:300
  86.5 1.5 %collective-permute-start.23 = (f32[256,512]{1,0:T(8,128)S(1)}, f32[256,512]{1,0:T(8,128)}, u32[]{:S(2)}, u32[]{:S(2)}) collective-permute-start(f32[256,512]{1,0:T(8,128)S(1)} %get-tuple-element.69), channel_id=1, source_target_pairs={{0,2},{8,10},{16,18},{24,26},{32,34},{40,42},{48,50},{56,58},{64,6... | collective-permute-start | bytes 1572872 | tf_op jit(solution)/shard_map/cond/branch_1_fun/ppermute | solution.py:300
  88.0 0.8 copy-done.6
  88.8 1.6 %add_select_fusion = f32[256,512]{1,0:T(8,128)S(1)} fusion(f32[256,512]{1,0:T(8,128)S(1)} %get-tuple-element.69, f32[256,512]{1,0:T(8,128)} %copy-done.6, f32[256,512]{1,0:T(8,128)} %collective-permute-done.22, f32[256,512]{1,0:T(8,128)} %collective-permute-done.23, pred[]{:T(512)S(6)} %eq.31), kind=kLoop, calls=%fused_computation.3 | loop fusion | flops 393216 | bytes 2621441 | tf_op jit(solution)/shard_map/cond/branch_1_fun/jit(_where)/select_n | solution.py:301
  90.4 1.3 %collective-permute-start.25 = (f32[256,512]{1,0:T(8,128)S(1)}, f32[256,512]{1,0:T(8,128)S(1)}, u32[]{:S(2)}, u32[]{:S(2)}) collective-permute-start(f32[256,512]{1,0:T(8,128)S(1)} %add_select_fusion), channel_id=1, source_target_pairs={{0,1},{2,3},{4,5},{6,7},{8,9},{10,11},{12,13},{14,15},{16,17},{18,... | collective-permute-start | bytes 1572872 | tf_op jit(solution)/shard_map/cond/branch_1_fun/ppermute | solution.py:302
  91.7 29.4 %collective-permute-done.25 = f32[256,512]{1,0:T(8,128)S(1)} collective-permute-done((f32[256,512]{1,0:T(8,128)S(1)}, f32[256,512]{1,0:T(8,128)S(1)}, u32[]{:S(2)}, u32[]{:S(2)}) %collective-permute-start.25) | collective-permute-done | bytes 524320 | tf_op jit(solution)/shard_map/cond/branch_1_fun/ppermute | solution.py:302
  121.2 2.3 %branch_1_fun.11 = f32[256,512]{1,0:T(8,128)S(1)} custom-call(s32[2]{0:T(128)S(1)} %get-tuple-element.49.place, s32[1,512]{1,0:T(1,128)S(1)} %copy-done.9, s32[8,512]{1,0:T(8,128)S(1)} %get-tuple-element.51.ranks_ref.refs_1_, f32[256,512]{1,0:T(8,128)S(1)} %get-tuple-element.52.refs_2_, f32[24,512]{1,0:T(8,128)S(1)} %get-tuple-element.58.refs_3_, ...), custom_call_target="tpu_custom_call" | custom-call | tf_op jit(solution)/shard_map/cond/branch_1_fun/pallas_call | solution.py:284
  123.6 0.8 copy-done.7
  (26 shorter events, 0.3 us)
Async XLA Ops:
  4.3 58.8 %copy-start.9 = (s32[1,512]{1,0:T(1,128)S(1)}, s32[1,512]{1,0:T(1,128)}, u32[]{:S(2)}) copy-start(s32[1,512]{1,0:T(1,128)} %get-tuple-element.50.piv_ref.refs_0_) | copy-start | bytes 6148 | tf_op jit(solution)/shard_map/cond
  4.4 77.2 %copy-start.2 = (f32[4,128,128]{2,1,0:T(8,128)S(1)}, f32[4,128,128]{2,1,0:T(8,128)}, u32[]{:S(2)}) copy-start(f32[4,128,128]{2,1,0:T(8,128)} %get-tuple-element.64.linv) | copy-start | bytes 786436 | tf_op jit(solution)/shard_map/cond
  4.4 77.2 %copy-start.4 = (f32[4,128,128]{2,1,0:T(8,128)S(1)}, f32[4,128,128]{2,1,0:T(8,128)}, u32[]{:S(2)}) copy-start(f32[4,128,128]{2,1,0:T(8,128)} %get-tuple-element.65.uinv) | copy-start | bytes 786436 | tf_op jit(solution)/shard_map/cond
  4.4 77.2 %copy-start.8 = (s32[512,8]{1,0:T(8,128)S(1)}, s32[512,8]{1,0:T(8,128)}, u32[]{:S(2)}) copy-start(s32[512,8]{1,0:T(8,128)} %get-tuple-element.62.cols_ref) | copy-start | bytes 49156 | tf_op jit(solution)/shard_map/cond
  4.4 54.1 %collective-permute-start.10 = (f32[96,512]{1,0:T(8,128)S(1)}, f32[96,512]{1,0:T(8,128)S(1)}, u32[]{:S(2)}, u32[]{:S(2)}) collective-permute-start(f32[96,512]{1,0:T(8,128)S(1)} %get-tuple-element.85), channel_id=1, source_target_pairs={{0,32},{8,40},{1,33},{9,41},{2,34},{10,42},{3,35},{11,43},{4,36},{... | collective-permute-start | bytes 589832 | tf_op jit(solution)/shard_map/cond/branch_1_fun/ppermute | solution.py:317
  5.2 57.8 %collective-permute-start.11 = (f32[96,512]{1,0:T(8,128)S(1)}, f32[96,512]{1,0:T(8,128)S(1)}, u32[]{:S(2)}, u32[]{:S(2)}) collective-permute-start(f32[96,512]{1,0:T(8,128)S(1)} %get-tuple-element.84), channel_id=1, source_target_pairs={{0,64},{8,72},{1,65},{9,73},{2,66},{10,74},{3,67},{11,75},{4,68},{... | collective-permute-start | bytes 589832 | tf_op jit(solution)/shard_map/cond/branch_1_fun/ppermute | solution.py:317
  5.9 57.2 %collective-permute-start.12 = (f32[96,512]{1,0:T(8,128)S(1)}, f32[96,512]{1,0:T(8,128)S(1)}, u32[]{:S(2)}, u32[]{:S(2)}) collective-permute-start(f32[96,512]{1,0:T(8,128)S(1)} %get-tuple-element.83), channel_id=1, source_target_pairs={{0,96},{8,104},{1,97},{9,105},{2,98},{10,106},{3,99},{11,107},{4,1... | collective-permute-start | bytes 589832 | tf_op jit(solution)/shard_map/cond/branch_1_fun/ppermute | solution.py:317
  54.6 25.6 %collective-permute-start.19 = (f32[176,512]{1,0:T(8,128)S(1)}, f32[176,512]{1,0:T(8,128)S(1)}, u32[]{:S(2)}, u32[]{:S(2)}) collective-permute-start(f32[176,512]{1,0:T(8,128)S(1)} %branch_1_fun.8.a0), channel_id=1, source_target_pairs={{0,128},{8,136},{16,144},{24,152},{32,160},{40,168},{48,176},{56,1... | collective-permute-start | bytes 1081352 | tf_op jit(solution)/shard_map/cond/branch_1_fun/ppermute | solution.py:295
  56.5 25.0 %collective-permute-start.20 = (f32[176,512]{1,0:T(8,128)S(1)}, f32[176,512]{1,0:T(8,128)S(1)}, u32[]{:S(2)}, u32[]{:S(2)}) collective-permute-start(f32[176,512]{1,0:T(8,128)S(1)} %branch_1_fun.8.a0), channel_id=1, source_target_pairs={{0,256},{8,264},{16,272},{24,280},{32,288},{40,296},{48,304},{56,3... | collective-permute-start | bytes 1081352 | tf_op jit(solution)/shard_map/cond/branch_1_fun/ppermute | solution.py:295
  58.5 23.0 %collective-permute-start.21 = (f32[176,512]{1,0:T(8,128)S(1)}, f32[176,512]{1,0:T(8,128)S(1)}, u32[]{:S(2)}, u32[]{:S(2)}) collective-permute-start(f32[176,512]{1,0:T(8,128)S(1)} %branch_1_fun.8.a0), channel_id=1, source_target_pairs={{0,384},{8,392},{16,400},{24,408},{32,416},{40,424},{48,432},{56,4... | collective-permute-start | bytes 1081352 | tf_op jit(solution)/shard_map/cond/branch_1_fun/ppermute | solution.py:295
  63.7 2.0 %collective-permute-start.13 = (f32[40,512]{1,0:T(8,128)S(1)}, f32[40,512]{1,0:T(8,128)S(1)}, u32[]{:S(2)}, u32[]{:S(2)}) collective-permute-start(f32[40,512]{1,0:T(8,128)S(1)} %get-tuple-element.55), channel_id=1, source_target_pairs={{0,8},{32,40},{64,72},{96,104},{8,0},{40,32},{72,64},{104,96},{1,9... | collective-permute-start | bytes 245768 | tf_op jit(solution)/shard_map/cond/branch_1_fun/ppermute | solution.py:324
  64.3 9.6 %collective-permute-start.14 = (f32[40,512]{1,0:T(8,128)S(1)}, f32[40,512]{1,0:T(8,128)S(1)}, u32[]{:S(2)}, u32[]{:S(2)}) collective-permute-start(f32[40,512]{1,0:T(8,128)S(1)} %get-tuple-element.56), channel_id=1, source_target_pairs={{0,16},{32,48},{64,80},{96,112},{8,24},{40,56},{72,88},{104,120},{... | collective-permute-start | bytes 245768 | tf_op jit(solution)/shard_map/cond/branch_1_fun/ppermute | solution.py:324
  65.6 10.7 %collective-permute-start.15 = (f32[40,512]{1,0:T(8,128)S(1)}, f32[40,512]{1,0:T(8,128)S(1)}, u32[]{:S(2)}, u32[]{:S(2)}) collective-permute-start(f32[40,512]{1,0:T(8,128)S(1)} %get-tuple-element.57), channel_id=1, source_target_pairs={{0,24},{32,56},{64,88},{96,120},{8,16},{40,48},{72,80},{104,112},{... | collective-permute-start | bytes 245768 | tf_op jit(solution)/shard_map/cond/branch_1_fun/ppermute | solution.py:324
  77.6 6.2 %collective-permute-start.16 = (f32[24,512]{1,0:T(8,128)S(1)}, f32[24,512]{1,0:T(8,128)S(1)}, u32[]{:S(2)}, u32[]{:S(2)}) collective-permute-start(f32[24,512]{1,0:T(8,128)S(1)} %get-tuple-element.59), channel_id=1, source_target_pairs={{0,128},{8,136},{16,144},{24,152},{32,160},{40,168},{48,176},{56,1... | collective-permute-start | bytes 147464 | tf_op jit(solution)/shard_map/cond/branch_1_fun/ppermute | solution.py:327
  78.9 4.9 %collective-permute-start.17 = (f32[24,512]{1,0:T(8,128)S(1)}, f32[24,512]{1,0:T(8,128)S(1)}, u32[]{:S(2)}, u32[]{:S(2)}) collective-permute-start(f32[24,512]{1,0:T(8,128)S(1)} %get-tuple-element.60), channel_id=1, source_target_pairs={{0,256},{8,264},{16,272},{24,280},{32,288},{40,296},{48,304},{56,3... | collective-permute-start | bytes 147464 | tf_op jit(solution)/shard_map/cond/branch_1_fun/ppermute | solution.py:327
  80.2 3.6 %collective-permute-start.18 = (f32[24,512]{1,0:T(8,128)S(1)}, f32[24,512]{1,0:T(8,128)S(1)}, u32[]{:S(2)}, u32[]{:S(2)}) collective-permute-start(f32[24,512]{1,0:T(8,128)S(1)} %get-tuple-element.61), channel_id=1, source_target_pairs={{0,384},{8,392},{16,400},{24,408},{32,416},{40,424},{48,432},{56,4... | collective-permute-start | bytes 147464 | tf_op jit(solution)/shard_map/cond/branch_1_fun/ppermute | solution.py:327
  84.4 3.7 %collective-permute-start.24 = (f32[256,512]{1,0:T(8,128)S(1)}, f32[256,512]{1,0:T(8,128)S(1)}, u32[]{:S(2)}, u32[]{:S(2)}) collective-permute-start(f32[256,512]{1,0:T(8,128)S(1)} %get-tuple-element.69), channel_id=1, source_target_pairs={{0,6},{8,14},{16,22},{24,30},{32,38},{40,46},{48,54},{56,62},{64,7... | collective-permute-start | bytes 1572872 | tf_op jit(solution)/shard_map/cond/branch_1_fun/ppermute | solution.py:300
  85.1 3.0 %collective-permute-start.22 = (f32[256,512]{1,0:T(8,128)S(1)}, f32[256,512]{1,0:T(8,128)}, u32[]{:S(2)}, u32[]{:S(2)}) collective-permute-start(f32[256,512]{1,0:T(8,128)S(1)} %get-tuple-element.69), channel_id=1, source_target_pairs={{0,4},{8,12},{16,20},{24,28},{32,36},{40,44},{48,52},{56,60},{64,6... | collective-permute-start | bytes 1572872 | tf_op jit(solution)/shard_map/cond/branch_1_fun/ppermute | solution.py:300
  86.5 2.3 %collective-permute-start.23 = (f32[256,512]{1,0:T(8,128)S(1)}, f32[256,512]{1,0:T(8,128)}, u32[]{:S(2)}, u32[]{:S(2)}) collective-permute-start(f32[256,512]{1,0:T(8,128)S(1)} %get-tuple-element.69), channel_id=1, source_target_pairs={{0,2},{8,10},{16,18},{24,26},{32,34},{40,42},{48,50},{56,58},{64,6... | collective-permute-start | bytes 1572872 | tf_op jit(solution)/shard_map/cond/branch_1_fun/ppermute | solution.py:300
  88.0 0.8 copy-start.6
  90.4 30.7 %collective-permute-start.25 = (f32[256,512]{1,0:T(8,128)S(1)}, f32[256,512]{1,0:T(8,128)S(1)}, u32[]{:S(2)}, u32[]{:S(2)}) collective-permute-start(f32[256,512]{1,0:T(8,128)S(1)} %add_select_fusion), channel_id=1, source_target_pairs={{0,1},{2,3},{4,5},{6,7},{8,9},{10,11},{12,13},{14,15},{16,17},{18,... | collective-permute-start | bytes 1572872 | tf_op jit(solution)/shard_map/cond/branch_1_fun/ppermute | solution.py:302
  123.6 0.8 copy-start.7

commit v2 on v1

v2 whole, which is shorter than its diff:
```python
import functools

import jax
import jax.numpy as jnp
from jax import lax
from jax.experimental import pallas as pl
from jax.experimental.pallas import tpu as pltpu
from jax.sharding import PartitionSpec as P

ROWS = 256
NB = 512
IB = 128
BLOCKS = NB // IB
XN = 4
ZN = 16
CAP_OWN = 24
CAP_X = 176
CAP_SX = 96
CAP_SXB = 40
CAP_SO = 16
PANEL = 1

VMEM = pl.BlockSpec(memory_space=pltpu.VMEM)
SMEM = pl.BlockSpec(memory_space=pltpu.SMEM)
ANY = pl.BlockSpec(memory_space=pl.ANY)
PARAMS = pltpu.CompilerParams(vmem_limit_bytes=48 * 1024 * 1024)
F32 = jnp.float32
BF16 = jnp.bfloat16


def two_parts(values):
    high = values.astype(BF16)
    return high, (values - high.astype(F32)).astype(BF16)


def product(left, right):
    left, left_low = two_parts(left)
    right, right_low = two_parts(right)
    small = jnp.dot(left, right_low, preferred_element_type=F32) + jnp.dot(
        left_low, right, preferred_element_type=F32
    )
    return jnp.dot(left, right, preferred_element_type=F32) + small


def exact_parts(values):
    high = values.astype(BF16)
    rest = values - high.astype(F32)
    middle = rest.astype(BF16)
    low = (rest - middle.astype(F32)).astype(BF16)
    return high, middle, low


def pick(chosen, values):
    high, middle, low = exact_parts(values)
    small = jnp.dot(chosen, middle, preferred_element_type=F32) + jnp.dot(
        chosen, low, preferred_element_type=F32
    )
    return jnp.dot(chosen, high, preferred_element_type=F32) + small


def ones_at(condition):
    return jnp.where(condition, F32(1.0), F32(0.0)).astype(BF16)


def match(slots, key, mask=None):
    rows = lax.broadcasted_iota(jnp.int32, (slots, key.shape[1]), 0)
    if mask is not None:
        key = jnp.where(mask, key, -1)
    return ones_at(rows == key)


def joined(target, source):
    both = lax.dot_general(target, source, (((1,), (1,)), ((), ())), preferred_element_type=F32)
    return both.astype(BF16)


def unpack(pivots):
    owner = pivots >> 8
    index = lax.broadcasted_iota(jnp.int32, pivots.shape, 1)
    return owner, pivots & 255, owner >> 4, owner & 15, index >> 8


def ranks_kernel(piv_ref, ranks_ref, cols_ref, ok_ref):
    owner, local, x_of, z_of, half = unpack(piv_ref[...])
    block = z_of >> 2
    keys = (
        (64, owner),
        (16, x_of),
        (16, half * 4 + x_of),
        (32, half * 16 + x_of * 4 + block),
        (128, half * 64 + owner),
    )
    classes = jnp.concatenate([match(count, key) for count, key in keys], axis=0)
    before = ones_at(
        lax.broadcasted_iota(jnp.int32, (NB, NB), 0) < lax.broadcasted_iota(jnp.int32, (NB, NB), 1)
    )
    counts = jnp.dot(classes, before, preferred_element_type=F32) * classes.astype(F32)
    ranks, start = [], 0
    for count, _ in keys:
        ranks.append(jnp.sum(counts[start : start + count], axis=0, keepdims=True))
        start += count
    fits = jnp.max(ranks[0]) < CAP_OWN
    for rank, cap in zip(ranks[1:], (CAP_X, CAP_SX, CAP_SXB, CAP_SO)):
        fits = fits & (jnp.max(rank) < cap)
    ok_ref[0] = jnp.where(fits, 1, 0).astype(jnp.int32)
    zero = jnp.zeros_like(ranks[0])
    ranks_ref[...] = jnp.concatenate(ranks + [zero] * 3, axis=0).astype(jnp.int32)
    wanted = jnp.concatenate(
        [x_of.astype(F32), jnp.minimum(ranks[1], 255.0)] + [zero] * 6, axis=0
    ).astype(BF16)
    diagonal = ones_at(
        lax.broadcasted_iota(jnp.int32, (NB, NB), 0) == lax.broadcasted_iota(jnp.int32, (NB, NB), 1)
    )
    cols_ref[...] = lax.dot_general(
        diagonal, wanted, (((1,), (1,)), ((), ())), preferred_element_type=F32
    ).astype(jnp.int32)


def pack_kernel(place, piv_ref, ranks_ref, mat_ref, asend_ref, m0, m1, m2, m3):
    row = place[0]
    owner, local, x_of, z_of, half = unpack(piv_ref[...])
    ranks = ranks_ref[...]
    chosen = joined(match(CAP_OWN, ranks[0:1], owner == row), match(ROWS, local))
    asend_ref[...] = pick(chosen, mat_ref[...])

    @pl.when(row < 2)
    def _():
        rank = jnp.where(row == 0, ranks[2:3, :ROWS], ranks[2:3, ROWS:])
        to = jnp.where(row == 0, x_of[:, :ROWS], x_of[:, ROWS:])
        chosen = jnp.concatenate([match(CAP_SX, rank, to == x) for x in range(XN)], axis=0)
        picked = pick(chosen, mat_ref[...])
        for x, out in enumerate((m0, m1, m2, m3)):
            out[...] = picked[x * CAP_SX : (x + 1) * CAP_SX]


def group_kernel(place, piv_ref, ranks_ref, gathered_ref, amsg_ref):
    row = place[0]
    owner, local, x_of, z_of, half = unpack(piv_ref[...])
    ranks = ranks_ref[...]
    target = match(CAP_X, ranks[1:2], x_of == (row >> 4))
    source = match(ZN * CAP_OWN, z_of * CAP_OWN + ranks[0:1])
    amsg_ref[...] = pick(joined(target, source), gathered_ref[...])


def far_kernel(place, piv_ref, ranks_ref, here_ref, r1, r2, r3, m0, m1, m2, m3):
    row = place[0]

    @pl.when((row & 15) < 2)
    def _():
        owner, local, x_of, z_of, half = unpack(piv_ref[...])
        ranks = ranks_ref[...]
        rows = jnp.where(row < 2, here_ref[...], r1[...] + r2[...] + r3[...])
        mine = (half == (row & 1)) & (x_of == (row >> 4))
        source = match(CAP_SX, ranks[2:3])
        target = jnp.concatenate(
            [match(CAP_SXB, ranks[3:4], mine & ((z_of >> 2) == block)) for block in range(4)], axis=0
        )
        picked = pick(joined(target, source), rows)
        for block, out in enumerate((m0, m1, m2, m3)):
            out[...] = picked[block * CAP_SXB : (block + 1) * CAP_SXB]


def near_kernel(place, piv_ref, ranks_ref, r0, r1, r2, r3, m0, m1, m2, m3):
    row = place[0]

    @pl.when((row & 3) >= 2)
    def _():
        owner, local, x_of, z_of, half = unpack(piv_ref[...])
        ranks = ranks_ref[...]
        side = row & 1
        rows = (r0[...] + r1[...]) + (r2[...] + r3[...])
        source = match(CAP_SXB, ranks[3:4])
        target = jnp.concatenate(
            [
                match(CAP_SO, ranks[4:5], (half == side) & (owner == (row & 60) + to))
                for to in (2 + side, 3 - side, side, 1 - side)
            ],
            axis=0,
        )
        picked = pick(joined(target, source), rows)
        for at, out in enumerate((m0, m1, m2, m3)):
            out[...] = picked[at * CAP_SO : (at + 1) * CAP_SO]


def factor(place, top_ref, linv_ref, uinv_ref, w_ref, v_ref, upper_ref):
    row = place[0]
    w_ref[...] = jnp.zeros((NB, NB), F32)
    v_ref[...] = jnp.zeros((NB, NB), F32)
    upper_ref[...] = jnp.zeros((ROWS, NB), F32)
    eye = jnp.where(
        lax.broadcasted_iota(jnp.int32, (IB, IB), 0) == lax.broadcasted_iota(jnp.int32, (IB, IB), 1),
        F32(1.0),
        F32(0.0),
    )
    for block in range(BLOCKS):
        begin, end = block * IB, (block + 1) * IB
        linv, uinv = linv_ref[block], uinv_ref[block]
        upper = product(linv, top_ref[begin:end, begin:])

        @pl.when(row == begin // ROWS)
        def _():
            upper_ref[begin % ROWS : begin % ROWS + IB, begin:] = upper

        if begin:
            v_left = product(linv, v_ref[begin:end, :begin])
            v_ref[begin:end, :begin] = v_left
            w_up = product(w_ref[:begin, begin:end], uinv)
            w_ref[:begin, begin:end] = w_up
        v_ref[begin:end, begin:end] = linv
        w_ref[begin:end, begin:end] = uinv
        if end < NB:
            lower = product(top_ref[end:, begin:end], uinv)
            top_ref[end:, end:] -= product(lower, upper[:, IB:])
            v_ref[end:, :end] -= product(lower, v_ref[begin:end, :end])
            w_ref[:end, end:] -= product(w_ref[:end, begin:end], upper[:, IB:])


def order_kernel(place, cols_ref, a0, a1, a2, a3, linv, uinv, top_ref, w_ref, v_ref, upper_ref, work):
    cols = cols_ref[...]
    slot = (((place[0] >> 4) - cols[:, 0:1]) & 3) * CAP_X + cols[:, 1:2]
    chosen = ones_at(lax.broadcasted_iota(jnp.int32, (NB, XN * CAP_X), 1) == slot)
    rows = jnp.concatenate([a0[...], a1[...], a2[...], a3[...]], axis=0)
    top = pick(chosen, rows)
    top_ref[...] = top

    @pl.when(place[1] == PANEL)
    def _():
        work[...] = top
        factor(place, work, linv, uinv, w_ref, v_ref, upper_ref)


def factor_kernel(place, top_ref, linv, uinv, w_ref, v_ref, upper_ref, work):
    @pl.when(place[1] == PANEL)
    def _():
        work[...] = top_ref[...]
        factor(place, work, linv, uinv, w_ref, v_ref, upper_ref)


def placed(row, piv_ref, ranks_ref, mat_ref, old):
    owner, local, x_of, z_of, half = unpack(piv_ref[...])
    mine = owner == row
    slot = ranks_ref[4:5] + jnp.where(half == (row & 1), 0, CAP_SO)
    chosen = joined(match(ROWS, local, mine), match(2 * CAP_SO, slot, mine))
    hit = jnp.sum(chosen.astype(F32), axis=1, keepdims=True) > 0.5
    return jnp.where(hit, pick(chosen, old), mat_ref[...])


def rows_kernel(moved, place, *refs):
    if moved:
        (piv_ref, ranks_ref, mat_ref, m0, r1, r2, r3, top_ref, w_ref, v_ref, upper_ref,
         qa_ref, qb_ref, qc_ref, panel_ref, old_ref) = refs
    else:
        mat_ref, top_ref, w_ref, v_ref, upper_ref, qa_ref, qb_ref, qc_ref, panel_ref = refs
    row, col = place[0], place[1]
    if moved:
        spot = row & 3
        old_ref[:CAP_SO] = jnp.where(spot >= 2, m0[...], r2[...])
        old_ref[CAP_SO:] = jnp.where(spot >= 2, r1[...], r3[...])

    @pl.when(col == 0)
    def _():
        qa_ref[...] = top_ref[:ROWS]
        qb_ref[...] = top_ref[ROWS:]
        if moved:
            qc_ref[: 2 * CAP_SO] = old_ref[...]
        else:
            qc_ref[...] = mat_ref[...]

    @pl.when((col == PANEL) & (row < 2))
    def _():
        q = -jnp.where(row == 0, v_ref[:ROWS], v_ref[ROWS:])
        for q_ref in (qa_ref, qb_ref, qc_ref):
            q_ref[...] = q
        panel_ref[...] = upper_ref[...]

    @pl.when((col == PANEL) & (row >= 2))
    def _():
        if moved:
            rows = placed(row, piv_ref, ranks_ref, mat_ref, old_ref[...])
        else:
            rows = mat_ref[...]
        half = NB // 2
        left = product(rows[:, :half], w_ref[:half, :half])
        right = product(rows, w_ref[:, half:])
        panel_ref[:, :half] = left
        panel_ref[:, half:] = right
        q_left = product(left, v_ref[:half, :half]) + product(right, v_ref[half:, :half])
        q_right = product(right, v_ref[half:, half:])
        for q_ref in (qa_ref, qb_ref, qc_ref):
            q_ref[:, :half] = q_left
            q_ref[:, half:] = q_right


def base_rows(moved, row, refs, more):
    rows = placed(row, *refs, more) if moved else more
    return jnp.where(row < 2, F32(0.0), rows)


def ready_kernel(moved, place, *refs):
    *rows_refs, more_ref, top_ref, base_ref, high_ref, low_ref = refs

    @pl.when(place[1] > 1)
    def _():
        base_ref[...] = base_rows(moved, place[0], rows_refs, more_ref[...])
        high_ref[...], low_ref[...] = two_parts(top_ref[...])


def final_kernel(moved, place, *refs):
    if moved:
        *rows_refs, out_ref, q_buf = refs
        rows_refs, refs = rows_refs[:3], (*rows_refs[3:], out_ref, q_buf)
    else:
        rows_refs = ()
    base_ref, high_ref, low_ref, panel_ref, *q_refs, out_ref, q_buf = refs
    row, col = place[0], place[1]

    @pl.when(col == 0)
    def _():
        out_ref[...] = panel_ref[...]

    for source, q_ref in zip((5, 3, 7, 4, 2, 6), q_refs[1:]):

        @pl.when(col == source)
        def _():
            q_buf[...] = q_ref[...]

    @pl.when(col == 1)
    def _():
        first, second, third = q_refs[1:4]
        more = third[: 2 * CAP_SO] if moved else third[...]
        q = q_refs[0][...]
        change = product(q[:, :ROWS], first[...]) + product(q[:, ROWS:], second[...])
        out_ref[...] = base_rows(moved, row, rows_refs, more) - change

    @pl.when(col > 1)
    def _():
        top = high_ref[...]
        q, q_low = two_parts(q_buf[...])
        change = jnp.dot(q, top, preferred_element_type=F32) + (
            jnp.dot(q, low_ref[...], preferred_element_type=F32)
            + jnp.dot(q_low, top, preferred_element_type=F32)
        )
        out_ref[...] = base_ref[...] - change


def shape(rows, cols=NB, dtype=F32):
    return jax.ShapeDtypeStruct((rows, cols), dtype)


def call(kernel, out_shape, *args, scratch=(), in_specs=None, out_specs=None):
    if in_specs is None:
        in_specs = [SMEM] + [VMEM] * (len(args) - 1)
    if out_specs is None:
        out_specs = jax.tree.map(lambda _: VMEM, out_shape)
    return pl.pallas_call(
        kernel,
        out_shape=out_shape,
        in_specs=in_specs,
        out_specs=out_specs,
        scratch_shapes=list(scratch),
        compiler_params=PARAMS,
    )(*args)


def shift_x(array, by):
    return lax.ppermute(array, "prow", [(i, (i + by * ZN) % (XN * ZN)) for i in range(XN * ZN)])


def swap_blocks(array):
    return lax.ppermute(array, "pcol", [(0, 1), (1, 0)] + [(k, k) for k in range(2, 8)])


def finish(moved, place, args, more, top, panel, messages):
    parts = [
        lax.ppermute(m, "pcol", [(PANEL, to), (0, PANEL)]) for m, to in zip(messages, (5, 3, 7))
    ]
    ready = call(
        functools.partial(ready_kernel, moved), [shape(ROWS), shape(NB, NB, BF16), shape(NB, NB, BF16)],
        place, *args, more, top,
    )
    first, ready = lax.optimization_barrier((parts[0], ready))
    hops = [
        lax.ppermute(part, "pcol", [(of, of - 1)])
        for part, of in zip((first, *parts[1:]), (5, 3, 7))
    ]
    panel, _ = lax.optimization_barrier((panel, first))
    panel = lax.ppermute(panel, "pcol", [(PANEL, 0)])
    return call(
        functools.partial(final_kernel, moved), shape(ROWS),
        place, *args, *ready, panel, messages[0], *parts, *hops,
        scratch=[pltpu.VMEM((ROWS, NB), F32)],
    )


Z_RINGS = [[x * ZN + z for z in range(ZN)] for x in range(XN)]
PAIRS = [(4 * a + 2, 4 * a + 3) for a in range(XN * ZN // 4)]
NEAR = [
    [(i, j) for i, j in PAIRS] + [(j, i) for i, j in PAIRS],
    [(i, i - 2) for i, j in PAIRS] + [(j, j - 2) for i, j in PAIRS],
    [(i, i - 1) for i, j in PAIRS] + [(j, j - 3) for i, j in PAIRS],
]


def direct(place, matrix, work, pivots, lower_inv, upper_inv, ranks, cols):
    asend, *old = call(
        pack_kernel, [shape(CAP_OWN)] + [shape(CAP_SX)] * 4, place, pivots, ranks, work
    )
    to_x = [
        lax.ppermute(old[x], "prow", [(s, x * ZN + s) for s in (0, 1)]) for x in (1, 3, 2)
    ]
    gathered = lax.all_gather(asend, "prow", axis_index_groups=Z_RINGS, tiled=True)
    gathered, old[0], to_x = lax.optimization_barrier((gathered, old[0], to_x))
    old = call(far_kernel, [shape(CAP_SXB)] * 4, place, pivots, ranks, old[0], *to_x)
    gathered, old = lax.optimization_barrier((gathered, old))
    to_block = [
        lax.ppermute(
            old[a], "prow", [(x * ZN + s, x * ZN + 4 * a + 2 + s) for x in range(XN) for s in (0, 1)]
        )
        for a in (0, 3, 1, 2)
    ]
    mine = call(group_kernel, shape(CAP_X), place, pivots, ranks, gathered)
    others = [shift_x(mine, by) for by in (1, 2, 3)]
    old = call(near_kernel, [shape(CAP_SO)] * 4, place, pivots, ranks, *to_block)
    near = [lax.ppermute(m, "prow", pairs) for m, pairs in zip(old[1:], NEAR)]
    top, w, v, upper = call(
        order_kernel, [shape(NB), shape(NB), shape(NB), shape(ROWS)],
        place, cols, mine, *others, lower_inv, upper_inv,
        scratch=[pltpu.VMEM((NB, NB), F32)],
    )
    *messages, panel, old = call(
        functools.partial(rows_kernel, True), [shape(ROWS)] * 4 + [shape(2 * CAP_SO)],
        place, pivots, ranks, work, old[0], *near, top, w, v, upper,
    )
    return finish(True, place, (pivots, ranks, matrix), old, top, panel, messages)


def general(place, matrix, work, pivots, lower_inv, upper_inv, ranks, cols):
    row = place[0]
    pivots = pivots[0]
    here = (pivots >> 8) == row
    local = pivots & 255
    index = jnp.arange(NB, dtype=jnp.int32)
    top_here = (index >> 8) == row
    both = jnp.concatenate(
        [
            jnp.where(here[:, None], work[local], F32(0.0)),
            jnp.where(top_here[:, None], work[index & 255], F32(0.0)),
        ],
        axis=0,
    )
    for bit in (1, 2, 4, 8, 16, 32):
        both = both + lax.ppermute(both, "prow", [(i, i ^ bit) for i in range(XN * ZN)])
    top, old = both[:NB], both[NB:]
    swapped = work.at[jnp.where(here, local, ROWS)].set(old, mode="drop")
    w, v, upper = call(
        factor_kernel, [shape(NB), shape(NB), shape(ROWS)],
        place, top, lower_inv, upper_inv,
        scratch=[pltpu.VMEM((NB, NB), F32)],
    )
    *messages, panel = call(
        functools.partial(rows_kernel, False), [shape(ROWS)] * 4,
        place, swapped, top, w, v, upper,
    )
    return finish(False, place, (), swapped, top, panel, messages)


def per_device(matrix, pivots, lower_inv, upper_inv):
    place = jnp.stack([lax.axis_index("prow"), lax.axis_index("pcol")]).astype(jnp.int32)
    pivots = pivots.reshape(1, NB)
    work = swap_blocks(matrix)
    ranks, cols, fits = call(
        ranks_kernel,
        [shape(8, NB, jnp.int32), shape(NB, 8, jnp.int32), jax.ShapeDtypeStruct((1,), jnp.int32)],
        pivots,
        in_specs=[VMEM],
        out_specs=[VMEM, VMEM, SMEM],
    )
    return lax.cond(
        fits[0] == 1, direct, general,
        place, matrix, work, pivots, lower_inv, upper_inv, ranks, cols,
    )


def solution(mesh):
    in_specs = (P("prow", "pcol"), P(), P(), P())
    out_specs = P("prow", "pcol")
    return jax.shard_map(
        per_device, mesh=mesh, in_specs=in_specs, out_specs=out_specs, check_vma=False
    )
```

time: 125 us -> 95.1 us (0.76)
  the two profiles are of different devices: /device:TPU:105 before, /device:TPU:1 now
where the time goes in v2:
time: 95.1 us; the launch traced here: 94.6 us
  starting transfers between devices  45.7 us (48%)
  blocking collectives  25.5 us (27%)
  Pallas kernels  15.1 us (16%)
  waiting for transfers between devices  6.19 us (7%)
    all_gather x1, blocking collectives, direct(): lax.all_gather(asend, 'prow', axis_index_groups=Z_RINGS, tiled=True)  25.5 us
    pallas_call x9, Pallas kernels, call(): pl.pallas_call(kernel, out_shape=out_shape, in_specs=in_specs, out_specs=...  15.1 us
    ppermute x3, starting transfers between devices, shift_x(): lax.ppermute(array, 'prow', [(i, (i + by * ZN) % (XN * ZN)) for i in rang...  10.7 us
    ppermute x1, starting transfers between devices, swap_blocks(): lax.ppermute(array, 'pcol', [(0, 1), (1, 0)] + [(k, k) for k in range(2,...  8.78 us
    ppermute x3, starting transfers between devices, finish(): lax.ppermute(m, 'pcol', [(PANEL, to), (0, PANEL)])  7 us
    ppermute x4, starting transfers between devices, direct(): lax.ppermute(old[a], 'prow', [(x * ZN + s, x * ZN + 4 * a + 2 + s) for x...  6.1 us
    ppermute x3, waiting for transfers between devices, finish(): lax.ppermute(m, 'pcol', [(PANEL, to), (0, PANEL)])  4.39 us
    ppermute x3, starting transfers between devices, direct(): lax.ppermute(old[x], 'prow', [(s, x * ZN + s) for s in (0, 1)])  3.9 us
  transfers between devices with their start and end apart: 21, of which 4 were waited for; matrix products, arithmetic and copies ran while one was open for 0% of the time, Pallas kernels for 9%

profile of v2, /device:TPU:1, one launch (start us, length us, event | category | flops | bytes accessed | tf_op | source)
XLA Modules:
  0.0 94.6 jit_solution(10399723189700467858)
XLA Ops:
  0.0 8.8 %collective-permute-start.33 = (f32[256,512]{1,0:T(8,128)}, f32[256,512]{1,0:T(8,128)S(1)}, u32[]{:S(2)}, u32[]{:S(2)}) collective-permute-start(f32[256,512]{1,0:T(8,128)} %param.6), channel_id=1, source_target_pairs={{0,1},{1,0},{2,2},{3,3},{4,4},{5,5},{6,6},{7,7},{8,9},{9,8},{10,10... | collective-permute-start | bytes 1572872 | tf_op jit(solution)/shard_map/ppermute | solution.py:370
  8.8 1.7 %shard_map.48 = (s32[8,512]{1,0:T(8,128)S(1)}, s32[512,8]{1,0:T(8,128)S(1)}, s32[1]{0:T(128)}) custom-call(s32[1,512]{1,0:T(1,128)} %bitcast.5), custom_call_target="tpu_custom_call" | custom-call | tf_op jit(solution)/shard_map/pallas_call | solution.py:355
  11.2 82.6 %conditional.1 = (f32[256,512]{1,0:T(8,128)S(1)}) conditional(s32[]{:T(128)} %bitcast.2, (s32[512]{0:T(512)}, s32[]{:T(128)}, f32[256,512]{1,0:T(8,128)S(1)}, s32[2]{0:T(128)S(1)}, f32[4,128,128]{2,1,0:T(8,128)}, /*index=5*/f32[4,128,128]{2,1,0:T(8,128)}) %tuple.17, (s32[2]{0:T(128)S(1)}, s32[1,512]{1,0:T(1,128)}, s32[8,512]{1,0:T(8,128)S(1)}, ...), branch_computations={%region_0.2_spmd, %region_2.3_spmd} | conditional | flops 4729856 | bytes 129528440 | solution.py:478
  11.4 1.8 %branch_1_fun.8 = (f32[24,512]{1,0:T(8,128)S(1)}, f32[96,512]{1,0:T(8,128)S(1)}, f32[96,512]{1,0:T(8,128)S(1)}, f32[96,512]{1,0:T(8,128)S(1)}, f32[96,512]{1,0:T(8,128)S(1)}) custom-call(s32[2]{0:T(128)S(1)} %get-tuple-element.57.place, s32[1,512]{1,0:T(1,128)} %get-tuple-element.58.piv_ref.refs_0_, s32[8,512]{1,0:T(8,128)S(1)} %get-tuple-element.59.ranks_ref.refs_1_, ...), custom_call_target="tpu_custom_call" | custom-call | tf_op jit(solution)/shard_map/cond/branch_1_fun/pallas_call | solution.py:355
  13.2 1.3 %collective-permute-start = (f32[96,512]{1,0:T(8,128)S(1)}, f32[96,512]{1,0:T(8,128)S(1)}, u32[]{:S(2)}, u32[]{:S(2)}) collective-permute-start(f32[96,512]{1,0:T(8,128)S(1)} %get-tuple-element.64), channel_id=1, source_target_pairs={{0,128},{8,136},{1,129},{9,137},{2,130},{10,138},{3,131},{11,139},... | collective-permute-start | bytes 589832 | tf_op jit(solution)/shard_map/cond/branch_1_fun/ppermute | solution.py:409
  14.5 1.3 %collective-permute-start.1 = (f32[96,512]{1,0:T(8,128)S(1)}, f32[96,512]{1,0:T(8,128)S(1)}, u32[]{:S(2)}, u32[]{:S(2)}) collective-permute-start(f32[96,512]{1,0:T(8,128)S(1)} %get-tuple-element.65), channel_id=1, source_target_pairs={{0,384},{8,392},{1,385},{9,393},{2,386},{10,394},{3,387},{11,395},... | collective-permute-start | bytes 589832 | tf_op jit(solution)/shard_map/cond/branch_1_fun/ppermute | solution.py:409
  15.8 1.3 %collective-permute-start.2 = (f32[96,512]{1,0:T(8,128)S(1)}, f32[96,512]{1,0:T(8,128)S(1)}, u32[]{:S(2)}, u32[]{:S(2)}) collective-permute-start(f32[96,512]{1,0:T(8,128)S(1)} %get-tuple-element.66), channel_id=1, source_target_pairs={{0,256},{8,264},{1,257},{9,265},{2,258},{10,266},{3,259},{11,267},... | collective-permute-start | bytes 589832 | tf_op jit(solution)/shard_map/cond/branch_1_fun/ppermute | solution.py:409
  17.2 25.5 %all_gather.2.gathered_ref = f32[384,512]{1,0:T(8,128)S(1)} all-gather(f32[24,512]{1,0:T(8,128)S(1)} %get-tuple-element.62), channel_id=1, replica_groups={{0,8,16,24,32,40,48,56,64,72,80,88,96,104,112,120},{128,136,144,152,160..., dimensions={0}, use_global_device_ids=true | all-gather | bytes 835584 | tf_op jit(solution)/shard_map/cond/branch_1_fun/all_gather | solution.py:411
  42.6 1.2 %branch_1_fun.9 = (f32[40,512]{1,0:T(8,128)S(1)}, f32[40,512]{1,0:T(8,128)S(1)}, f32[40,512]{1,0:T(8,128)S(1)}, f32[40,512]{1,0:T(8,128)S(1)}) custom-call(s32[2]{0:T(128)S(1)} %get-tuple-element.57.place, s32[1,512]{1,0:T(1,128)} %get-tuple-element.58.piv_ref.refs_0_, s32[8,512]{1,0:T(8,128)S(1)} %get-tuple-element.59.ranks_ref.refs_1_, ...), custom_call_target="tpu_custom_call" | custom-call | tf_op jit(solution)/shard_map/cond/branch_1_fun/pallas_call | solution.py:355
  43.8 1.3 %branch_1_fun.11.a0 = f32[176,512]{1,0:T(8,128)S(1)} custom-call(s32[2]{0:T(128)S(1)} %get-tuple-element.57.place, s32[1,512]{1,0:T(1,128)S(1)} %copy-done.7, s32[8,512]{1,0:T(8,128)S(1)} %get-tuple-element.59.ranks_ref.refs_1_, f32[384,512]{1,0:T(8,128)S(1)} %all_gather.2.gathered_ref), custom_call_target="tpu_custom_call" | custom-call | tf_op jit(solution)/shard_map/cond/branch_1_fun/pallas_call | solution.py:355
  45.1 3.3 %collective-permute-start.10 = (f32[176,512]{1,0:T(8,128)S(1)}, f32[176,512]{1,0:T(8,128)S(1)}, u32[]{:S(2)}, u32[]{:S(2)}) collective-permute-start(f32[176,512]{1,0:T(8,128)S(1)} %branch_1_fun.11.a0), channel_id=1, source_target_pairs={{0,128},{8,136},{16,144},{24,152},{32,160},{40,168},{48,176},{56,1... | collective-permute-start | bytes 1081352 | tf_op jit(solution)/shard_map/cond/branch_1_fun/ppermute | solution.py:366
  48.4 4.3 %collective-permute-start.11 = (f32[176,512]{1,0:T(8,128)S(1)}, f32[176,512]{1,0:T(8,128)S(1)}, u32[]{:S(2)}, u32[]{:S(2)}) collective-permute-start(f32[176,512]{1,0:T(8,128)S(1)} %branch_1_fun.11.a0), channel_id=1, source_target_pairs={{0,256},{8,264},{16,272},{24,280},{32,288},{40,296},{48,304},{56,3... | collective-permute-start | bytes 1081352 | tf_op jit(solution)/shard_map/cond/branch_1_fun/ppermute | solution.py:366
  52.8 3.1 %collective-permute-start.12 = (f32[176,512]{1,0:T(8,128)S(1)}, f32[176,512]{1,0:T(8,128)S(1)}, u32[]{:S(2)}, u32[]{:S(2)}) collective-permute-start(f32[176,512]{1,0:T(8,128)S(1)} %branch_1_fun.11.a0), channel_id=1, source_target_pairs={{0,384},{8,392},{16,400},{24,408},{32,416},{40,424},{48,432},{56,4... | collective-permute-start | bytes 1081352 | tf_op jit(solution)/shard_map/cond/branch_1_fun/ppermute | solution.py:366
  55.9 1.4 %collective-permute-start.3 = (f32[40,512]{1,0:T(8,128)S(1)}, f32[40,512]{1,0:T(8,128)S(1)}, u32[]{:S(2)}, u32[]{:S(2)}) collective-permute-start(f32[40,512]{1,0:T(8,128)S(1)} %get-tuple-element.76), channel_id=1, source_target_pairs={{0,16},{8,24},{128,144},{136,152},{256,272},{264,280},{384,400},{3... | collective-permute-start | bytes 245768 | tf_op jit(solution)/shard_map/cond/branch_1_fun/ppermute | solution.py:416
  57.3 1.8 %collective-permute-start.4 = (f32[40,512]{1,0:T(8,128)S(1)}, f32[40,512]{1,0:T(8,128)S(1)}, u32[]{:S(2)}, u32[]{:S(2)}) collective-permute-start(f32[40,512]{1,0:T(8,128)S(1)} %get-tuple-element.77), channel_id=1, source_target_pairs={{0,112},{8,120},{128,240},{136,248},{256,368},{264,376},{384,496},... | collective-permute-start | bytes 245768 | tf_op jit(solution)/shard_map/cond/branch_1_fun/ppermute | solution.py:416
  59.1 1.4 %collective-permute-start.5 = (f32[40,512]{1,0:T(8,128)S(1)}, f32[40,512]{1,0:T(8,128)S(1)}, u32[]{:S(2)}, u32[]{:S(2)}) collective-permute-start(f32[40,512]{1,0:T(8,128)S(1)} %get-tuple-element.78), channel_id=1, source_target_pairs={{0,48},{8,56},{128,176},{136,184},{256,304},{264,312},{384,432},{3... | collective-permute-start | bytes 245768 | tf_op jit(solution)/shard_map/cond/branch_1_fun/ppermute | solution.py:416
  60.8 1.4 %collective-permute-start.6 = (f32[40,512]{1,0:T(8,128)S(1)}, f32[40,512]{1,0:T(8,128)S(1)}, u32[]{:S(2)}, u32[]{:S(2)}) collective-permute-start(f32[40,512]{1,0:T(8,128)S(1)} %get-tuple-element.79), channel_id=1, source_target_pairs={{0,80},{8,88},{128,208},{136,216},{256,336},{264,344},{384,464},{3... | collective-permute-start | bytes 245768 | tf_op jit(solution)/shard_map/cond/branch_1_fun/ppermute | solution.py:416
  62.3 1.5 %collective-permute-done.6.r3 = f32[40,512]{1,0:T(8,128)S(1)} collective-permute-done((f32[40,512]{1,0:T(8,128)S(1)}, f32[40,512]{1,0:T(8,128)S(1)}, u32[]{:S(2)}, u32[]{:S(2)}) %collective-permute-start.6) | collective-permute-done | bytes 81952 | tf_op jit(solution)/shard_map/cond/branch_1_fun/ppermute | solution.py:416
  65.0 1.3 %collective-permute-start.8 = (f32[16,512]{1,0:T(8,128)S(1)}, f32[16,512]{1,0:T(8,128)S(1)}, u32[]{:S(2)}, u32[]{:S(2)}) collective-permute-start(f32[16,512]{1,0:T(8,128)S(1)} %get-tuple-element.82), channel_id=1, source_target_pairs={{16,0},{48,32},{80,64},{112,96},{144,128},{176,160},{208,192},{240... | collective-permute-start | bytes 98312 | tf_op jit(solution)/shard_map/cond/branch_1_fun/ppermute | solution.py:424
  66.3 1.3 %collective-permute-start.9 = (f32[16,512]{1,0:T(8,128)S(1)}, f32[16,512]{1,0:T(8,128)S(1)}, u32[]{:S(2)}, u32[]{:S(2)}) collective-permute-start(f32[16,512]{1,0:T(8,128)S(1)} %get-tuple-element.83), channel_id=1, source_target_pairs={{16,8},{48,40},{80,72},{112,104},{144,136},{176,168},{208,200},{24... | collective-permute-start | bytes 98312 | tf_op jit(solution)/shard_map/cond/branch_1_fun/ppermute | solution.py:424
  67.6 5.5 %branch_1_fun.12 = (f32[512,512]{1,0:T(8,128)S(1)}, f32[512,512]{1,0:T(8,128)S(1)}, f32[512,512]{1,0:T(8,128)S(1)}, f32[256,512]{1,0:T(8,128)S(1)}) custom-call(s32[2]{0:T(128)S(1)} %get-tuple-element.57.place, s32[512,8]{1,0:T(8,128)S(1)} %get-tuple-element.84.cols_ref, f32[176,512]{1,0:T(8,128)S(1)} %branch_1_fun.11.a0, ...), custom_call_target="tpu_custom_call" | custom-call | tf_op jit(solution)/shard_map/cond/branch_1_fun/pallas_call | solution.py:355
  73.2 0.7 branch_1_fun.13
  73.9 3.2 %collective-permute-start.13 = (f32[256,512]{1,0:T(8,128)S(1)}, f32[256,512]{1,0:T(8,128)S(1)}, u32[]{:S(2)}, u32[]{:S(2)}) collective-permute-start(f32[256,512]{1,0:T(8,128)S(1)} %get-tuple-element.92.refs_7_), channel_id=1, source_target_pairs={{1,5},{0,1},{9,13},{8,9},{17,21},{16,17},{25,29},{24,25},{33,37},{... | collective-permute-start | bytes 1572872 | tf_op jit(solution)/shard_map/cond/branch_1_fun/ppermute | solution.py:375
  77.0 1.9 %collective-permute-start.15 = (f32[256,512]{1,0:T(8,128)S(1)}, f32[256,512]{1,0:T(8,128)S(1)}, u32[]{:S(2)}, u32[]{:S(2)}) collective-permute-start(f32[256,512]{1,0:T(8,128)S(1)} %get-tuple-element.103), channel_id=1, source_target_pairs={{1,3},{0,1},{9,11},{8,9},{17,19},{16,17},{25,27},{24,25},{33,35},{... | collective-permute-start | bytes 1572872 | tf_op jit(solution)/shard_map/cond/branch_1_fun/ppermute | solution.py:375
  79.0 1.9 %collective-permute-start.16 = (f32[256,512]{1,0:T(8,128)S(1)}, f32[256,512]{1,0:T(8,128)S(1)}, u32[]{:S(2)}, u32[]{:S(2)}) collective-permute-start(f32[256,512]{1,0:T(8,128)S(1)} %get-tuple-element.104), channel_id=1, source_target_pairs={{1,7},{0,1},{9,15},{8,9},{17,23},{16,17},{25,31},{24,25},{33,39},{... | collective-permute-start | bytes 1572872 | tf_op jit(solution)/shard_map/cond/branch_1_fun/ppermute | solution.py:375
  81.5 4.4 %collective-permute-done.13.refs_8_ = f32[256,512]{1,0:T(8,128)S(1)} collective-permute-done((f32[256,512]{1,0:T(8,128)S(1)}, f32[256,512]{1,0:T(8,128)S(1)}, u32[]{:S(2)}, u32[]{:S(2)}) %collective-permute-start.13) | collective-permute-done | bytes 524320 | tf_op jit(solution)/shard_map/cond/branch_1_fun/ppermute | solution.py:375
  85.8 0.7 collective-permute-start.17
  86.5 3.8 %collective-permute-start.14 = (f32[256,512]{1,0:T(8,128)S(1)}, f32[256,512]{1,0:T(8,128)S(1)}, u32[]{:S(2)}, u32[]{:S(2)}) collective-permute-start(f32[256,512]{1,0:T(8,128)S(1)} %get-tuple-element.102), channel_id=1, source_target_pairs={{1,0},{9,8},{17,16},{25,24},{33,32},{41,40},{49,48},{57,56},{65,64... | collective-permute-start | bytes 1572872 | tf_op jit(solution)/shard_map/cond/branch_1_fun/ppermute | solution.py:387
  90.4 0.7 collective-permute-start.18
  91.1 0.7 collective-permute-start.19
  91.9 1.9 %branch_1_fun.15 = f32[256,512]{1,0:T(8,128)S(1)} custom-call(s32[2]{0:T(128)S(1)} %get-tuple-element.57.place, s32[1,512]{1,0:T(1,128)S(1)} %copy-done.7, s32[8,512]{1,0:T(8,128)S(1)} %get-tuple-element.59.ranks_ref.refs_1_, f32[256,512]{1,0:T(8,128)S(1)} %copy-done.1, f32[256,512]{1,0:T(8,128)S(1)} %get-tuple-element.97.refs_3_, ...), custom_call_target="tpu_custom_call" | custom-call | tf_op jit(solution)/shard_map/cond/branch_1_fun/pallas_call | solution.py:355
  93.8 0.8 copy-done.6
  (32 shorter events, 2.2 us)
Async XLA Ops:
  0.0 11.2 %collective-permute-start.33 = (f32[256,512]{1,0:T(8,128)}, f32[256,512]{1,0:T(8,128)S(1)}, u32[]{:S(2)}, u32[]{:S(2)}) collective-permute-start(f32[256,512]{1,0:T(8,128)} %param.6), channel_id=1, source_target_pairs={{0,1},{1,0},{2,2},{3,3},{4,4},{5,5},{6,6},{7,7},{8,9},{9,8},{10,10... | collective-permute-start | bytes 1572872 | tf_op jit(solution)/shard_map/ppermute | solution.py:370
  11.4 32.4 %copy-start.7 = (s32[1,512]{1,0:T(1,128)S(1)}, s32[1,512]{1,0:T(1,128)}, u32[]{:S(2)}) copy-start(s32[1,512]{1,0:T(1,128)} %get-tuple-element.58.piv_ref.refs_0_) | copy-start | bytes 6148 | tf_op jit(solution)/shard_map/cond
  11.4 56.2 %copy-start.3 = (f32[4,128,128]{2,1,0:T(8,128)S(1)}, f32[4,128,128]{2,1,0:T(8,128)}, u32[]{:S(2)}) copy-start(f32[4,128,128]{2,1,0:T(8,128)} %get-tuple-element.86.linv) | copy-start | bytes 786436 | tf_op jit(solution)/shard_map/cond
  11.4 56.2 %copy-start.5 = (f32[4,128,128]{2,1,0:T(8,128)S(1)}, f32[4,128,128]{2,1,0:T(8,128)}, u32[]{:S(2)}) copy-start(f32[4,128,128]{2,1,0:T(8,128)} %get-tuple-element.87.uinv) | copy-start | bytes 786436 | tf_op jit(solution)/shard_map/cond
  13.2 29.4 %collective-permute-start = (f32[96,512]{1,0:T(8,128)S(1)}, f32[96,512]{1,0:T(8,128)S(1)}, u32[]{:S(2)}, u32[]{:S(2)}) collective-permute-start(f32[96,512]{1,0:T(8,128)S(1)} %get-tuple-element.64), channel_id=1, source_target_pairs={{0,128},{8,136},{1,129},{9,137},{2,130},{10,138},{3,131},{11,139},... | collective-permute-start | bytes 589832 | tf_op jit(solution)/shard_map/cond/branch_1_fun/ppermute | solution.py:409
  14.5 28.1 %collective-permute-start.1 = (f32[96,512]{1,0:T(8,128)S(1)}, f32[96,512]{1,0:T(8,128)S(1)}, u32[]{:S(2)}, u32[]{:S(2)}) collective-permute-start(f32[96,512]{1,0:T(8,128)S(1)} %get-tuple-element.65), channel_id=1, source_target_pairs={{0,384},{8,392},{1,385},{9,393},{2,386},{10,394},{3,387},{11,395},... | collective-permute-start | bytes 589832 | tf_op jit(solution)/shard_map/cond/branch_1_fun/ppermute | solution.py:409
  15.8 26.8 %collective-permute-start.2 = (f32[96,512]{1,0:T(8,128)S(1)}, f32[96,512]{1,0:T(8,128)S(1)}, u32[]{:S(2)}, u32[]{:S(2)}) collective-permute-start(f32[96,512]{1,0:T(8,128)S(1)} %get-tuple-element.66), channel_id=1, source_target_pairs={{0,256},{8,264},{1,257},{9,265},{2,258},{10,266},{3,259},{11,267},... | collective-permute-start | bytes 589832 | tf_op jit(solution)/shard_map/cond/branch_1_fun/ppermute | solution.py:409
  45.1 21.1 %collective-permute-start.10 = (f32[176,512]{1,0:T(8,128)S(1)}, f32[176,512]{1,0:T(8,128)S(1)}, u32[]{:S(2)}, u32[]{:S(2)}) collective-permute-start(f32[176,512]{1,0:T(8,128)S(1)} %branch_1_fun.11.a0), channel_id=1, source_target_pairs={{0,128},{8,136},{16,144},{24,152},{32,160},{40,168},{48,176},{56,1... | collective-permute-start | bytes 1081352 | tf_op jit(solution)/shard_map/cond/branch_1_fun/ppermute | solution.py:366
  48.4 19.1 %collective-permute-start.11 = (f32[176,512]{1,0:T(8,128)S(1)}, f32[176,512]{1,0:T(8,128)S(1)}, u32[]{:S(2)}, u32[]{:S(2)}) collective-permute-start(f32[176,512]{1,0:T(8,128)S(1)} %branch_1_fun.11.a0), channel_id=1, source_target_pairs={{0,256},{8,264},{16,272},{24,280},{32,288},{40,296},{48,304},{56,3... | collective-permute-start | bytes 1081352 | tf_op jit(solution)/shard_map/cond/branch_1_fun/ppermute | solution.py:366
  52.8 14.8 %collective-permute-start.12 = (f32[176,512]{1,0:T(8,128)S(1)}, f32[176,512]{1,0:T(8,128)S(1)}, u32[]{:S(2)}, u32[]{:S(2)}) collective-permute-start(f32[176,512]{1,0:T(8,128)S(1)} %branch_1_fun.11.a0), channel_id=1, source_target_pairs={{0,384},{8,392},{16,400},{24,408},{32,416},{40,424},{48,432},{56,4... | collective-permute-start | bytes 1081352 | tf_op jit(solution)/shard_map/cond/branch_1_fun/ppermute | solution.py:366
  55.9 3.2 %collective-permute-start.3 = (f32[40,512]{1,0:T(8,128)S(1)}, f32[40,512]{1,0:T(8,128)S(1)}, u32[]{:S(2)}, u32[]{:S(2)}) collective-permute-start(f32[40,512]{1,0:T(8,128)S(1)} %get-tuple-element.76), channel_id=1, source_target_pairs={{0,16},{8,24},{128,144},{136,152},{256,272},{264,280},{384,400},{3... | collective-permute-start | bytes 245768 | tf_op jit(solution)/shard_map/cond/branch_1_fun/ppermute | solution.py:416
  57.3 3.5 %collective-permute-start.4 = (f32[40,512]{1,0:T(8,128)S(1)}, f32[40,512]{1,0:T(8,128)S(1)}, u32[]{:S(2)}, u32[]{:S(2)}) collective-permute-start(f32[40,512]{1,0:T(8,128)S(1)} %get-tuple-element.77), channel_id=1, source_target_pairs={{0,112},{8,120},{128,240},{136,248},{256,368},{264,376},{384,496},... | collective-permute-start | bytes 245768 | tf_op jit(solution)/shard_map/cond/branch_1_fun/ppermute | solution.py:416
  59.1 3.2 %collective-permute-start.5 = (f32[40,512]{1,0:T(8,128)S(1)}, f32[40,512]{1,0:T(8,128)S(1)}, u32[]{:S(2)}, u32[]{:S(2)}) collective-permute-start(f32[40,512]{1,0:T(8,128)S(1)} %get-tuple-element.78), channel_id=1, source_target_pairs={{0,48},{8,56},{128,176},{136,184},{256,304},{264,312},{384,432},{3... | collective-permute-start | bytes 245768 | tf_op jit(solution)/shard_map/cond/branch_1_fun/ppermute | solution.py:416
  60.8 2.9 %collective-permute-start.6 = (f32[40,512]{1,0:T(8,128)S(1)}, f32[40,512]{1,0:T(8,128)S(1)}, u32[]{:S(2)}, u32[]{:S(2)}) collective-permute-start(f32[40,512]{1,0:T(8,128)S(1)} %get-tuple-element.79), channel_id=1, source_target_pairs={{0,80},{8,88},{128,208},{136,216},{256,336},{264,344},{384,464},{3... | collective-permute-start | bytes 245768 | tf_op jit(solution)/shard_map/cond/branch_1_fun/ppermute | solution.py:416
  64.3 8.8 %collective-permute-start.7 = (f32[16,512]{1,0:T(8,128)S(1)}, f32[16,512]{1,0:T(8,128)S(1)}, u32[]{:S(2)}, u32[]{:S(2)}) collective-permute-start(f32[16,512]{1,0:T(8,128)S(1)} %get-tuple-element.81), channel_id=1, source_target_pairs={{16,24},{48,56},{80,88},{112,120},{144,152},{176,184},{208,216},{2... | collective-permute-start | bytes 98312 | tf_op jit(solution)/shard_map/cond/branch_1_fun/ppermute | solution.py:424
  65.0 8.2 %collective-permute-start.8 = (f32[16,512]{1,0:T(8,128)S(1)}, f32[16,512]{1,0:T(8,128)S(1)}, u32[]{:S(2)}, u32[]{:S(2)}) collective-permute-start(f32[16,512]{1,0:T(8,128)S(1)} %get-tuple-element.82), channel_id=1, source_target_pairs={{16,0},{48,32},{80,64},{112,96},{144,128},{176,160},{208,192},{240... | collective-permute-start | bytes 98312 | tf_op jit(solution)/shard_map/cond/branch_1_fun/ppermute | solution.py:424
  66.3 6.9 %collective-permute-start.9 = (f32[16,512]{1,0:T(8,128)S(1)}, f32[16,512]{1,0:T(8,128)S(1)}, u32[]{:S(2)}, u32[]{:S(2)}) collective-permute-start(f32[16,512]{1,0:T(8,128)S(1)} %get-tuple-element.83), channel_id=1, source_target_pairs={{16,8},{48,40},{80,72},{112,104},{144,136},{176,168},{208,200},{24... | collective-permute-start | bytes 98312 | tf_op jit(solution)/shard_map/cond/branch_1_fun/ppermute | solution.py:424
  73.1 7.8 %copy-start.1 = (f32[256,512]{1,0:T(8,128)S(1)}, f32[256,512]{1,0:T(8,128)}, u32[]{:S(2)}) copy-start(f32[256,512]{1,0:T(8,128)} %get-tuple-element.60.refs_2_) | copy-start | bytes 1572868 | tf_op jit(solution)/shard_map/cond
  73.9 12.0 %collective-permute-start.13 = (f32[256,512]{1,0:T(8,128)S(1)}, f32[256,512]{1,0:T(8,128)S(1)}, u32[]{:S(2)}, u32[]{:S(2)}) collective-permute-start(f32[256,512]{1,0:T(8,128)S(1)} %get-tuple-element.92.refs_7_), channel_id=1, source_target_pairs={{1,5},{0,1},{9,13},{8,9},{17,21},{16,17},{25,29},{24,25},{33,37},{... | collective-permute-start | bytes 1572872 | tf_op jit(solution)/shard_map/cond/branch_1_fun/ppermute | solution.py:375
  77.0 13.3 %collective-permute-start.15 = (f32[256,512]{1,0:T(8,128)S(1)}, f32[256,512]{1,0:T(8,128)S(1)}, u32[]{:S(2)}, u32[]{:S(2)}) collective-permute-start(f32[256,512]{1,0:T(8,128)S(1)} %get-tuple-element.103), channel_id=1, source_target_pairs={{1,3},{0,1},{9,11},{8,9},{17,19},{16,17},{25,27},{24,25},{33,35},{... | collective-permute-start | bytes 1572872 | tf_op jit(solution)/shard_map/cond/branch_1_fun/ppermute | solution.py:375
  79.0 12.1 %collective-permute-start.16 = (f32[256,512]{1,0:T(8,128)S(1)}, f32[256,512]{1,0:T(8,128)S(1)}, u32[]{:S(2)}, u32[]{:S(2)}) collective-permute-start(f32[256,512]{1,0:T(8,128)S(1)} %get-tuple-element.104), channel_id=1, source_target_pairs={{1,7},{0,1},{9,15},{8,9},{17,23},{16,17},{25,31},{24,25},{33,39},{... | collective-permute-start | bytes 1572872 | tf_op jit(solution)/shard_map/cond/branch_1_fun/ppermute | solution.py:375
  85.8 6.0 %collective-permute-start.17 = (f32[256,512]{1,0:T(8,128)S(1)}, f32[256,512]{1,0:T(8,128)S(1)}, u32[]{:S(2)}, u32[]{:S(2)}) collective-permute-start(f32[256,512]{1,0:T(8,128)S(1)} %collective-permute-done.13.refs_8_), channel_id=1, source_target_pairs={{5,4},{13,12},{21,20},{29,28},{37,36},{45,44},{53,52},{61,60},{69,... | collective-permute-start | bytes 1572872 | tf_op jit(solution)/shard_map/cond/branch_1_fun/ppermute | solution.py:383
  86.5 5.3 %collective-permute-start.14 = (f32[256,512]{1,0:T(8,128)S(1)}, f32[256,512]{1,0:T(8,128)S(1)}, u32[]{:S(2)}, u32[]{:S(2)}) collective-permute-start(f32[256,512]{1,0:T(8,128)S(1)} %get-tuple-element.102), channel_id=1, source_target_pairs={{1,0},{9,8},{17,16},{25,24},{33,32},{41,40},{49,48},{57,56},{65,64... | collective-permute-start | bytes 1572872 | tf_op jit(solution)/shard_map/cond/branch_1_fun/ppermute | solution.py:387
  90.4 1.5 %collective-permute-start.18 = (f32[256,512]{1,0:T(8,128)S(1)}, f32[256,512]{1,0:T(8,128)S(1)}, u32[]{:S(2)}, u32[]{:S(2)}) collective-permute-start(f32[256,512]{1,0:T(8,128)S(1)} %collective-permute-done.15.refs_9_), channel_id=1, source_target_pairs={{3,2},{11,10},{19,18},{27,26},{35,34},{43,42},{51,50},{59,58},{67,... | collective-permute-start | bytes 1572872 | tf_op jit(solution)/shard_map/cond/branch_1_fun/ppermute | solution.py:383
  91.1 0.8 collective-permute-start.19
  93.8 0.8 copy-start.6

commit v3 on v2

--- a/solution.py
+++ b/solution.py
@@ -91,29 +91,36 @@
         (128, half * 64 + owner),
     )
     classes = jnp.concatenate([match(count, key) for count, key in keys], axis=0)
-    before = ones_at(
-        lax.broadcasted_iota(jnp.int32, (NB, NB), 0) < lax.broadcasted_iota(jnp.int32, (NB, NB), 1)
-    )
-    counts = jnp.dot(classes, before, preferred_element_type=F32) * classes.astype(F32)
-    ranks, start = [], 0
-    for count, _ in keys:
-        ranks.append(jnp.sum(counts[start : start + count], axis=0, keepdims=True))
-        start += count
-    fits = jnp.max(ranks[0]) < CAP_OWN
-    for rank, cap in zip(ranks[1:], (CAP_X, CAP_SX, CAP_SXB, CAP_SO)):
-        fits = fits & (jnp.max(rank) < cap)
+    rows = lax.broadcasted_iota(jnp.int32, (IB, 2 * IB), 0)
+    lanes = lax.broadcasted_iota(jnp.int32, (IB, 2 * IB), 1)
+    counter = ones_at((rows < lanes) | (lanes >= IB))
+    passed, pieces = jnp.zeros((classes.shape[0], IB), F32), []
+    for block in range(BLOCKS):
+        held = classes[:, block * IB : (block + 1) * IB]
+        count = jnp.dot(held, counter, preferred_element_type=F32)
+        counts = (count[:, :IB] + passed) * held.astype(F32)
+        passed = passed + count[:, IB:]
+        start, piece = 0, []
+        for size, _ in keys:
+            piece.append(jnp.sum(counts[start : start + size], axis=0, keepdims=True))
+            start += size
+        pieces.append(jnp.concatenate(piece + [jnp.zeros((3, IB), F32)], axis=0))
+    ranks = jnp.concatenate(pieces, axis=1)
+    fits = jnp.max(ranks[0:1]) < CAP_OWN
+    for at, cap in enumerate((CAP_X, CAP_SX, CAP_SXB, CAP_SO)):
+        fits = fits & (jnp.max(ranks[at + 1 : at + 2]) < cap)
     ok_ref[0] = jnp.where(fits, 1, 0).astype(jnp.int32)
-    zero = jnp.zeros_like(ranks[0])
-    ranks_ref[...] = jnp.concatenate(ranks + [zero] * 3, axis=0).astype(jnp.int32)
+    ranks_ref[...] = ranks.astype(jnp.int32)
+    zero = jnp.zeros((6, NB), F32)
     wanted = jnp.concatenate(
-        [x_of.astype(F32), jnp.minimum(ranks[1], 255.0)] + [zero] * 6, axis=0
+        [x_of.astype(F32), jnp.minimum(ranks[1:2], 255.0), zero], axis=0
     ).astype(BF16)
-    diagonal = ones_at(
-        lax.broadcasted_iota(jnp.int32, (NB, NB), 0) == lax.broadcasted_iota(jnp.int32, (NB, NB), 1)
-    )
-    cols_ref[...] = lax.dot_general(
-        diagonal, wanted, (((1,), (1,)), ((), ())), preferred_element_type=F32
-    ).astype(jnp.int32)
+    diagonal = ones_at(rows[:, :IB] == lanes[:, :IB])
+    for block in range(BLOCKS):
+        part = slice(block * IB, (block + 1) * IB)
+        cols_ref[part] = lax.dot_general(
+            diagonal, wanted[:, part], (((1,), (1,)), ((), ())), preferred_element_type=F32
+        ).astype(jnp.int32)
 
 
 def pack_kernel(place, piv_ref, ranks_ref, mat_ref, asend_ref, m0, m1, m2, m3):
@@ -133,24 +140,21 @@
             out[...] = picked[x * CAP_SX : (x + 1) * CAP_SX]
 
 
-def group_kernel(place, piv_ref, ranks_ref, gathered_ref, amsg_ref):
+def group_kernel(
+    place, piv_ref, ranks_ref, gathered_ref, here_ref, r1, r2, r3, amsg_ref, m0, m1, m2, m3
+):
     row = place[0]
     owner, local, x_of, z_of, half = unpack(piv_ref[...])
     ranks = ranks_ref[...]
-    target = match(CAP_X, ranks[1:2], x_of == (row >> 4))
+    in_x = x_of == (row >> 4)
+    target = match(CAP_X, ranks[1:2], in_x)
     source = match(ZN * CAP_OWN, z_of * CAP_OWN + ranks[0:1])
     amsg_ref[...] = pick(joined(target, source), gathered_ref[...])
 
-
-def far_kernel(place, piv_ref, ranks_ref, here_ref, r1, r2, r3, m0, m1, m2, m3):
-    row = place[0]
-
     @pl.when((row & 15) < 2)
     def _():
-        owner, local, x_of, z_of, half = unpack(piv_ref[...])
-        ranks = ranks_ref[...]
         rows = jnp.where(row < 2, here_ref[...], r1[...] + r2[...] + r3[...])
-        mine = (half == (row & 1)) & (x_of == (row >> 4))
+        mine = (half == (row & 1)) & in_x
         source = match(CAP_SX, ranks[2:3])
         target = jnp.concatenate(
             [match(CAP_SXB, ranks[3:4], mine & ((z_of >> 2) == block)) for block in range(4)], axis=0
@@ -220,7 +224,10 @@
     slot = (((place[0] >> 4) - cols[:, 0:1]) & 3) * CAP_X + cols[:, 1:2]
     chosen = ones_at(lax.broadcasted_iota(jnp.int32, (NB, XN * CAP_X), 1) == slot)
     rows = jnp.concatenate([a0[...], a1[...], a2[...], a3[...]], axis=0)
-    top = pick(chosen, rows)
+    high, low = two_parts(rows)
+    top = jnp.dot(chosen, high, preferred_element_type=F32) + jnp.dot(
+        chosen, low, preferred_element_type=F32
+    )
     top_ref[...] = top
 
     @pl.when(place[1] == PANEL)
@@ -247,10 +254,10 @@
 
 def rows_kernel(moved, place, *refs):
     if moved:
-        (piv_ref, ranks_ref, mat_ref, m0, r1, r2, r3, top_ref, w_ref, v_ref, upper_ref,
-         qa_ref, qb_ref, qc_ref, panel_ref, old_ref) = refs
+        (piv_ref, ranks_ref, mat_ref, m0, r1, r2, r3, w_ref, v_ref, upper_ref,
+         q_ref, panel_ref, old_ref) = refs
     else:
-        mat_ref, top_ref, w_ref, v_ref, upper_ref, qa_ref, qb_ref, qc_ref, panel_ref = refs
+        mat_ref, w_ref, v_ref, upper_ref, q_ref, panel_ref = refs
     row, col = place[0], place[1]
     if moved:
         spot = row & 3
@@ -259,18 +266,14 @@
 
     @pl.when(col == 0)
     def _():
-        qa_ref[...] = top_ref[:ROWS]
-        qb_ref[...] = top_ref[ROWS:]
         if moved:
-            qc_ref[: 2 * CAP_SO] = old_ref[...]
+            q_ref[: 2 * CAP_SO] = old_ref[...]
         else:
-            qc_ref[...] = mat_ref[...]
+            q_ref[...] = mat_ref[...]
 
     @pl.when((col == PANEL) & (row < 2))
     def _():
-        q = -jnp.where(row == 0, v_ref[:ROWS], v_ref[ROWS:])
-        for q_ref in (qa_ref, qb_ref, qc_ref):
-            q_ref[...] = q
+        q_ref[...] = -jnp.where(row == 0, v_ref[:ROWS], v_ref[ROWS:])
         panel_ref[...] = upper_ref[...]
 
     @pl.when((col == PANEL) & (row >= 2))
@@ -284,11 +287,8 @@
         right = product(rows, w_ref[:, half:])
         panel_ref[:, :half] = left
         panel_ref[:, half:] = right
-        q_left = product(left, v_ref[:half, :half]) + product(right, v_ref[half:, :half])
-        q_right = product(right, v_ref[half:, half:])
-        for q_ref in (qa_ref, qb_ref, qc_ref):
-            q_ref[:, :half] = q_left
-            q_ref[:, half:] = q_right
+        q_ref[:, :half] = product(left, v_ref[:half, :half]) + product(right, v_ref[half:, :half])
+        q_ref[:, half:] = product(right, v_ref[half:, half:])
 
 
 def base_rows(moved, row, refs, more):
@@ -305,32 +305,33 @@
         high_ref[...], low_ref[...] = two_parts(top_ref[...])
 
 
+def pass_kernel(place, a_ref, b_ref, c_ref, panel_ref, out_ref):
+    for source, ref in ((5, a_ref), (3, b_ref), (7, c_ref), (PANEL, panel_ref)):
+
+        @pl.when(place[1] == source)
+        def _():
+            out_ref[...] = ref[...]
+
+
 def final_kernel(moved, place, *refs):
-    if moved:
-        *rows_refs, out_ref, q_buf = refs
-        rows_refs, refs = rows_refs[:3], (*rows_refs[3:], out_ref, q_buf)
-    else:
-        rows_refs = ()
-    base_ref, high_ref, low_ref, panel_ref, *q_refs, out_ref, q_buf = refs
+    rows_refs, refs = refs[: 3 * moved], refs[3 * moved :]
+    base_ref, high_ref, low_ref, top_ref, q_ref, a_ref, b_ref, c_ref, hop_ref, out_ref, q_buf = refs
     row, col = place[0], place[1]
 
     @pl.when(col == 0)
     def _():
-        out_ref[...] = panel_ref[...]
-
-    for source, q_ref in zip((5, 3, 7, 4, 2, 6), q_refs[1:]):
-
-        @pl.when(col == source)
+        out_ref[...] = hop_ref[...]
+
+    @pl.when(col == 1)
+    def _():
+        more = a_ref[: 2 * CAP_SO] if moved else a_ref[...]
+        out_ref[...] = base_rows(moved, row, rows_refs, more) - product(q_ref[...], top_ref[...])
+
+    for sources, ref in (((5,), a_ref), ((3,), b_ref), ((7,), c_ref), ((2, 4, 6), hop_ref)):
+
+        @pl.when(functools.reduce(jnp.logical_or, [col == source for source in sources]))
         def _():
-            q_buf[...] = q_ref[...]
-
-    @pl.when(col == 1)
-    def _():
-        first, second, third = q_refs[1:4]
-        more = third[: 2 * CAP_SO] if moved else third[...]
-        q = q_refs[0][...]
-        change = product(q[:, :ROWS], first[...]) + product(q[:, ROWS:], second[...])
-        out_ref[...] = base_rows(moved, row, rows_refs, more) - change
+            q_buf[...] = ref[...]
 
     @pl.when(col > 1)
     def _():
@@ -370,24 +371,22 @@
     return lax.ppermute(array, "pcol", [(0, 1), (1, 0)] + [(k, k) for k in range(2, 8)])
 
 
-def finish(moved, place, args, more, top, panel, messages):
+def finish(moved, place, args, more, top, panel, message):
+    top_moved = lax.ppermute(top, "pcol", [(0, PANEL)])
     parts = [
-        lax.ppermute(m, "pcol", [(PANEL, to), (0, PANEL)]) for m, to in zip(messages, (5, 3, 7))
+        lax.ppermute(message, "pcol", pairs)
+        for pairs in ([(PANEL, 5), (0, PANEL)], [(PANEL, 3)], [(PANEL, 7)])
     ]
     ready = call(
         functools.partial(ready_kernel, moved), [shape(ROWS), shape(NB, NB, BF16), shape(NB, NB, BF16)],
         place, *args, more, top,
     )
-    first, ready = lax.optimization_barrier((parts[0], ready))
-    hops = [
-        lax.ppermute(part, "pcol", [(of, of - 1)])
-        for part, of in zip((first, *parts[1:]), (5, 3, 7))
-    ]
-    panel, _ = lax.optimization_barrier((panel, first))
-    panel = lax.ppermute(panel, "pcol", [(PANEL, 0)])
+    parts, ready = lax.optimization_barrier((parts, ready))
+    onward = call(pass_kernel, shape(ROWS), place, *parts, panel)
+    hop = lax.ppermute(onward, "pcol", [(5, 4), (3, 2), (7, 6), (PANEL, 0)])
     return call(
         functools.partial(final_kernel, moved), shape(ROWS),
-        place, *args, *ready, panel, messages[0], *parts, *hops,
+        place, *args, *ready, top_moved, message, *parts, hop,
         scratch=[pltpu.VMEM((ROWS, NB), F32)],
     )
 
@@ -409,16 +408,16 @@
         lax.ppermute(old[x], "prow", [(s, x * ZN + s) for s in (0, 1)]) for x in (1, 3, 2)
     ]
     gathered = lax.all_gather(asend, "prow", axis_index_groups=Z_RINGS, tiled=True)
-    gathered, old[0], to_x = lax.optimization_barrier((gathered, old[0], to_x))
-    old = call(far_kernel, [shape(CAP_SXB)] * 4, place, pivots, ranks, old[0], *to_x)
-    gathered, old = lax.optimization_barrier((gathered, old))
+    mine, *old = call(
+        group_kernel, [shape(CAP_X)] + [shape(CAP_SXB)] * 4,
+        place, pivots, ranks, gathered, old[0], *to_x,
+    )
     to_block = [
         lax.ppermute(
             old[a], "prow", [(x * ZN + s, x * ZN + 4 * a + 2 + s) for x in range(XN) for s in (0, 1)]
         )
         for a in (0, 3, 1, 2)
     ]
-    mine = call(group_kernel, shape(CAP_X), place, pivots, ranks, gathered)
     others = [shift_x(mine, by) for by in (1, 2, 3)]
     old = call(near_kernel, [shape(CAP_SO)] * 4, place, pivots, ranks, *to_block)
     near = [lax.ppermute(m, "prow", pairs) for m, pairs in zip(old[1:], NEAR)]
@@ -427,11 +426,11 @@
         place, cols, mine, *others, lower_inv, upper_inv,
         scratch=[pltpu.VMEM((NB, NB), F32)],
     )
-    *messages, panel, old = call(
-        functools.partial(rows_kernel, True), [shape(ROWS)] * 4 + [shape(2 * CAP_SO)],
-        place, pivots, ranks, work, old[0], *near, top, w, v, upper,
-    )
-    return finish(True, place, (pivots, ranks, matrix), old, top, panel, messages)
+    message, panel, old = call(
+        functools.partial(rows_kernel, True), [shape(ROWS), shape(ROWS), shape(2 * CAP_SO)],
+        place, pivots, ranks, work, old[0], *near, w, v, upper,
+    )
+    return finish(True, place, (pivots, ranks, matrix), old, top, panel, message)
 
 
 def general(place, matrix, work, pivots, lower_inv, upper_inv, ranks, cols):
@@ -457,11 +456,10 @@
         place, top, lower_inv, upper_inv,
         scratch=[pltpu.VMEM((NB, NB), F32)],
     )
-    *messages, panel = call(
-        functools.partial(rows_kernel, False), [shape(ROWS)] * 4,
-        place, swapped, top, w, v, upper,
-    )
-    return finish(False, place, (), swapped, top, panel, messages)
+    message, panel = call(
+        functools.partial(rows_kernel, False), [shape(ROWS)] * 2, place, swapped, w, v, upper
+    )
+    return finish(False, place, (), swapped, top, panel, message)
 
 
 def per_device(matrix, pivots, lower_inv, upper_inv):

time: 95.1 us -> 94.4 us (level)
  waiting for transfers between devices: 6.19 us -> 10.7 us
  starting transfers between devices: 45.7 us -> 41.4 us
    ppermute x7 -> x5, starting transfers between devices: 12.9 us -> 8.6 us  [the longest x3 5.99 us: finish(): lax.ppermute(message, 'pcol', pairs)]
    ppermute x7 -> x5, waiting for transfers between devices: 4.46 us -> 8.67 us  [the longest x3 7.19 us: finish(): lax.ppermute(message, 'pcol', pairs)]
  transfers between devices with their start and end apart: 21 -> 19, of which waited for: 4 -> 6; matrix products, arithmetic and copies ran while one was open for 0% -> 0% of each run, Pallas kernels for 9% -> 9%
where the time goes in v3:
time: 94.4 us; the launch traced here: 93.9 us
  starting transfers between devices  41.4 us (44%)
  blocking collectives  25.4 us (27%)
  Pallas kernels  14.3 us (15%)
  waiting for transfers between devices  10.7 us (11%)
    all_gather x1, blocking collectives, direct(): lax.all_gather(asend, 'prow', axis_index_groups=Z_RINGS, tiled=True)  25.4 us
    pallas_call x9, Pallas kernels, call(): pl.pallas_call(kernel, out_shape=out_shape, in_specs=in_specs, out_specs=...  14.3 us
    ppermute x3, starting transfers between devices, shift_x(): lax.ppermute(array, 'prow', [(i, (i + by * ZN) % (XN * ZN)) for i in rang...  10.7 us
    ppermute x1, starting transfers between devices, swap_blocks(): lax.ppermute(array, 'pcol', [(0, 1), (1, 0)] + [(k, k) for k in range(2,...  8.78 us
    ppermute x3, waiting for transfers between devices, finish(): lax.ppermute(message, 'pcol', pairs)  7.19 us
    ppermute x4, starting transfers between devices, direct(): lax.ppermute(old[a], 'prow', [(x * ZN + s, x * ZN + 4 * a + 2 + s) for x...  6.15 us
    ppermute x3, starting transfers between devices, finish(): lax.ppermute(message, 'pcol', pairs)  5.99 us
    ppermute x3, starting transfers between devices, direct(): lax.ppermute(old[x], 'prow', [(s, x * ZN + s) for s in (0, 1)])  3.9 us
  transfers between devices with their start and end apart: 19, of which 6 were waited for; matrix products, arithmetic and copies ran while one was open for 0% of the time, Pallas kernels for 9%

profile of v3, /device:TPU:1, one launch (start us, length us, event | category | flops | bytes accessed | tf_op | source)
XLA Modules:
  0.0 93.9 jit_solution(7768855534149108283)
XLA Ops:
  0.0 8.8 %collective-permute-start.29 = (f32[256,512]{1,0:T(8,128)}, f32[256,512]{1,0:T(8,128)S(1)}, u32[]{:S(2)}, u32[]{:S(2)}) collective-permute-start(f32[256,512]{1,0:T(8,128)} %param.6), channel_id=1, source_target_pairs={{0,1},{1,0},{2,2},{3,3},{4,4},{5,5},{6,6},{7,7},{8,9},{9,8},{10,10... | collective-permute-start | bytes 1572872 | tf_op jit(solution)/shard_map/ppermute | solution.py:371
  8.8 1.6 %shard_map.48 = (s32[8,512]{1,0:T(8,128)S(1)}, s32[512,8]{1,0:T(8,128)S(1)}, s32[1]{0:T(128)}) custom-call(s32[1,512]{1,0:T(1,128)} %bitcast.5), custom_call_target="tpu_custom_call" | custom-call | tf_op jit(solution)/shard_map/pallas_call | solution.py:356
  11.2 81.9 %conditional.1 = (f32[256,512]{1,0:T(8,128)S(1)}) conditional(s32[]{:T(128)} %bitcast.2, (s32[512]{0:T(512)}, s32[]{:T(128)}, f32[256,512]{1,0:T(8,128)S(1)}, s32[2]{0:T(128)S(1)}, f32[4,128,128]{2,1,0:T(8,128)}, /*index=5*/f32[4,128,128]{2,1,0:T(8,128)}) %tuple.13, (s32[2]{0:T(128)S(1)}, s32[1,512]{1,0:T(1,128)}, s32[8,512]{1,0:T(8,128)S(1)}, ...), branch_computations={%region_0.2_spmd, %region_2.3_spmd} | conditional | flops 4729856 | bytes 127431200 | solution.py:476
  11.4 1.8 %branch_1_fun.8 = (f32[24,512]{1,0:T(8,128)S(1)}, f32[96,512]{1,0:T(8,128)S(1)}, f32[96,512]{1,0:T(8,128)S(1)}, f32[96,512]{1,0:T(8,128)S(1)}, f32[96,512]{1,0:T(8,128)S(1)}) custom-call(s32[2]{0:T(128)S(1)} %get-tuple-element.56.place, s32[1,512]{1,0:T(1,128)} %get-tuple-element.57.piv_ref.refs_0_, s32[8,512]{1,0:T(8,128)S(1)} %get-tuple-element.58.ranks_ref.refs_1_, ...), custom_call_target="tpu_custom_call" | custom-call | tf_op jit(solution)/shard_map/cond/branch_1_fun/pallas_call | solution.py:356
  13.2 1.3 %collective-permute-start = (f32[96,512]{1,0:T(8,128)S(1)}, f32[96,512]{1,0:T(8,128)S(1)}, u32[]{:S(2)}, u32[]{:S(2)}) collective-permute-start(f32[96,512]{1,0:T(8,128)S(1)} %get-tuple-element.63), channel_id=1, source_target_pairs={{0,128},{8,136},{1,129},{9,137},{2,130},{10,138},{3,131},{11,139},... | collective-permute-start | bytes 589832 | tf_op jit(solution)/shard_map/cond/branch_1_fun/ppermute | solution.py:408
  14.5 1.3 %collective-permute-start.1 = (f32[96,512]{1,0:T(8,128)S(1)}, f32[96,512]{1,0:T(8,128)S(1)}, u32[]{:S(2)}, u32[]{:S(2)}) collective-permute-start(f32[96,512]{1,0:T(8,128)S(1)} %get-tuple-element.64), channel_id=1, source_target_pairs={{0,384},{8,392},{1,385},{9,393},{2,386},{10,394},{3,387},{11,395},... | collective-permute-start | bytes 589832 | tf_op jit(solution)/shard_map/cond/branch_1_fun/ppermute | solution.py:408
  15.8 1.3 %collective-permute-start.2 = (f32[96,512]{1,0:T(8,128)S(1)}, f32[96,512]{1,0:T(8,128)S(1)}, u32[]{:S(2)}, u32[]{:S(2)}) collective-permute-start(f32[96,512]{1,0:T(8,128)S(1)} %get-tuple-element.65), channel_id=1, source_target_pairs={{0,256},{8,264},{1,257},{9,265},{2,258},{10,266},{3,259},{11,267},... | collective-permute-start | bytes 589832 | tf_op jit(solution)/shard_map/cond/branch_1_fun/ppermute | solution.py:408
  17.1 25.4 %all_gather.2.gathered_ref = f32[384,512]{1,0:T(8,128)S(1)} all-gather(f32[24,512]{1,0:T(8,128)S(1)} %get-tuple-element.61), channel_id=1, replica_groups={{0,8,16,24,32,40,48,56,64,72,80,88,96,104,112,120},{128,136,144,152,160..., dimensions={0}, use_global_device_ids=true | all-gather | bytes 835584 | tf_op jit(solution)/shard_map/cond/branch_1_fun/all_gather | solution.py:410
  42.6 1.9 %branch_1_fun.9 = (f32[176,512]{1,0:T(8,128)S(1)}, f32[40,512]{1,0:T(8,128)S(1)}, f32[40,512]{1,0:T(8,128)S(1)}, f32[40,512]{1,0:T(8,128)S(1)}, f32[40,512]{1,0:T(8,128)S(1)}) custom-call(s32[2]{0:T(128)S(1)} %get-tuple-element.56.place, s32[1,512]{1,0:T(1,128)} %get-tuple-element.57.piv_ref.refs_0_, s32[8,512]{1,0:T(8,128)S(1)} %get-tuple-element.58.ranks_ref.refs_1_, ...), custom_call_target="tpu_custom_call" | custom-call | tf_op jit(solution)/shard_map/cond/branch_1_fun/pallas_call | solution.py:356
  44.5 3.3 %collective-permute-start.10 = (f32[176,512]{1,0:T(8,128)S(1)}, f32[176,512]{1,0:T(8,128)S(1)}, u32[]{:S(2)}, u32[]{:S(2)}) collective-permute-start(f32[176,512]{1,0:T(8,128)S(1)} %get-tuple-element.75.a0), channel_id=1, source_target_pairs={{0,128},{8,136},{16,144},{24,152},{32,160},{40,168},{48,176},{56,1... | collective-permute-start | bytes 1081352 | tf_op jit(solution)/shard_map/cond/branch_1_fun/ppermute | solution.py:367
  47.9 4.3 %collective-permute-start.11 = (f32[176,512]{1,0:T(8,128)S(1)}, f32[176,512]{1,0:T(8,128)S(1)}, u32[]{:S(2)}, u32[]{:S(2)}) collective-permute-start(f32[176,512]{1,0:T(8,128)S(1)} %get-tuple-element.75.a0), channel_id=1, source_target_pairs={{0,256},{8,264},{16,272},{24,280},{32,288},{40,296},{48,304},{56,3... | collective-permute-start | bytes 1081352 | tf_op jit(solution)/shard_map/cond/branch_1_fun/ppermute | solution.py:367
  52.2 3.1 %collective-permute-start.12 = (f32[176,512]{1,0:T(8,128)S(1)}, f32[176,512]{1,0:T(8,128)S(1)}, u32[]{:S(2)}, u32[]{:S(2)}) collective-permute-start(f32[176,512]{1,0:T(8,128)S(1)} %get-tuple-element.75.a0), channel_id=1, source_target_pairs={{0,384},{8,392},{16,400},{24,408},{32,416},{40,424},{48,432},{56,4... | collective-permute-start | bytes 1081352 | tf_op jit(solution)/shard_map/cond/branch_1_fun/ppermute | solution.py:367
  55.3 1.4 %collective-permute-start.3 = (f32[40,512]{1,0:T(8,128)S(1)}, f32[40,512]{1,0:T(8,128)S(1)}, u32[]{:S(2)}, u32[]{:S(2)}) collective-permute-start(f32[40,512]{1,0:T(8,128)S(1)} %get-tuple-element.66), channel_id=1, source_target_pairs={{0,16},{8,24},{128,144},{136,152},{256,272},{264,280},{384,400},{3... | collective-permute-start | bytes 245768 | tf_op jit(solution)/shard_map/cond/branch_1_fun/ppermute | solution.py:416
  56.7 1.8 %collective-permute-start.4 = (f32[40,512]{1,0:T(8,128)S(1)}, f32[40,512]{1,0:T(8,128)S(1)}, u32[]{:S(2)}, u32[]{:S(2)}) collective-permute-start(f32[40,512]{1,0:T(8,128)S(1)} %get-tuple-element.67), channel_id=1, source_target_pairs={{0,112},{8,120},{128,240},{136,248},{256,368},{264,376},{384,496},... | collective-permute-start | bytes 245768 | tf_op jit(solution)/shard_map/cond/branch_1_fun/ppermute | solution.py:416
  58.5 1.5 %collective-permute-start.5 = (f32[40,512]{1,0:T(8,128)S(1)}, f32[40,512]{1,0:T(8,128)S(1)}, u32[]{:S(2)}, u32[]{:S(2)}) collective-permute-start(f32[40,512]{1,0:T(8,128)S(1)} %get-tuple-element.68), channel_id=1, source_target_pairs={{0,48},{8,56},{128,176},{136,184},{256,304},{264,312},{384,432},{3... | collective-permute-start | bytes 245768 | tf_op jit(solution)/shard_map/cond/branch_1_fun/ppermute | solution.py:416
  60.2 1.5 %collective-permute-start.6 = (f32[40,512]{1,0:T(8,128)S(1)}, f32[40,512]{1,0:T(8,128)S(1)}, u32[]{:S(2)}, u32[]{:S(2)}) collective-permute-start(f32[40,512]{1,0:T(8,128)S(1)} %get-tuple-element.69), channel_id=1, source_target_pairs={{0,80},{8,88},{128,208},{136,216},{256,336},{264,344},{384,464},{3... | collective-permute-start | bytes 245768 | tf_op jit(solution)/shard_map/cond/branch_1_fun/ppermute | solution.py:416
  61.7 1.5 %collective-permute-done.6.r3 = f32[40,512]{1,0:T(8,128)S(1)} collective-permute-done((f32[40,512]{1,0:T(8,128)S(1)}, f32[40,512]{1,0:T(8,128)S(1)}, u32[]{:S(2)}, u32[]{:S(2)}) %collective-permute-start.6) | collective-permute-done | bytes 81952 | tf_op jit(solution)/shard_map/cond/branch_1_fun/ppermute | solution.py:416
  63.7 0.7 collective-permute-start.7
  64.4 1.3 %collective-permute-start.8 = (f32[16,512]{1,0:T(8,128)S(1)}, f32[16,512]{1,0:T(8,128)S(1)}, u32[]{:S(2)}, u32[]{:S(2)}) collective-permute-start(f32[16,512]{1,0:T(8,128)S(1)} %get-tuple-element.72), channel_id=1, source_target_pairs={{16,0},{48,32},{80,64},{112,96},{144,128},{176,160},{208,192},{240... | collective-permute-start | bytes 98312 | tf_op jit(solution)/shard_map/cond/branch_1_fun/ppermute | solution.py:423
  65.7 1.3 %collective-permute-start.9 = (f32[16,512]{1,0:T(8,128)S(1)}, f32[16,512]{1,0:T(8,128)S(1)}, u32[]{:S(2)}, u32[]{:S(2)}) collective-permute-start(f32[16,512]{1,0:T(8,128)S(1)} %get-tuple-element.73), channel_id=1, source_target_pairs={{16,8},{48,40},{80,72},{112,104},{144,136},{176,168},{208,200},{24... | collective-permute-start | bytes 98312 | tf_op jit(solution)/shard_map/cond/branch_1_fun/ppermute | solution.py:423
  67.0 5.1 %branch_1_fun.11 = (f32[512,512]{1,0:T(8,128)S(1)}, f32[512,512]{1,0:T(8,128)S(1)}, f32[512,512]{1,0:T(8,128)S(1)}, f32[256,512]{1,0:T(8,128)S(1)}) custom-call(s32[2]{0:T(128)S(1)} %get-tuple-element.56.place, s32[512,8]{1,0:T(8,128)S(1)} %get-tuple-element.74.cols_ref, f32[176,512]{1,0:T(8,128)S(1)} %get-tuple-element.75.a0, ...), custom_call_target="tpu_custom_call" | custom-call | tf_op jit(solution)/shard_map/cond/branch_1_fun/pallas_call | solution.py:356
  72.4 0.6 branch_1_fun.12
  73.1 3.3 %collective-permute-start.13 = (f32[256,512]{1,0:T(8,128)S(1)}, f32[256,512]{1,0:T(8,128)S(1)}, u32[]{:S(2)}, u32[]{:S(2)}) collective-permute-start(f32[256,512]{1,0:T(8,128)S(1)} %get-tuple-element.81.refs_7_), channel_id=1, source_target_pairs={{1,5},{0,1},{9,13},{8,9},{17,21},{16,17},{25,29},{24,25},{33,37},{... | collective-permute-start | bytes 1572872 | tf_op jit(solution)/shard_map/cond/branch_1_fun/ppermute | solution.py:377
  76.5 1.3 %collective-permute-start.14 = (f32[256,512]{1,0:T(8,128)S(1)}, f32[256,512]{1,0:T(8,128)S(1)}, u32[]{:S(2)}, u32[]{:S(2)}) collective-permute-start(f32[256,512]{1,0:T(8,128)S(1)} %get-tuple-element.81.refs_7_), channel_id=1, source_target_pairs={{1,3},{9,11},{17,19},{25,27},{33,35},{41,43},{49,51},{57,59},{65,6... | collective-permute-start | bytes 1572872 | tf_op jit(solution)/shard_map/cond/branch_1_fun/ppermute | solution.py:377
  77.8 1.3 %collective-permute-start.15 = (f32[256,512]{1,0:T(8,128)S(1)}, f32[256,512]{1,0:T(8,128)S(1)}, u32[]{:S(2)}, u32[]{:S(2)}) collective-permute-start(f32[256,512]{1,0:T(8,128)S(1)} %get-tuple-element.81.refs_7_), channel_id=1, source_target_pairs={{1,7},{9,15},{17,23},{25,31},{33,39},{41,47},{49,55},{57,63},{65,7... | collective-permute-start | bytes 1572872 | tf_op jit(solution)/shard_map/cond/branch_1_fun/ppermute | solution.py:377
  79.1 1.3 %collective-permute-start.16 = (f32[512,512]{1,0:T(8,128)S(1)}, f32[512,512]{1,0:T(8,128)S(1)}, u32[]{:S(2)}, u32[]{:S(2)}) collective-permute-start(f32[512,512]{1,0:T(8,128)S(1)} %get-tuple-element.83.refs_4_), channel_id=1, source_target_pairs={{0,1},{8,9},{16,17},{24,25},{32,33},{40,41},{48,49},{56,57},{64,65... | collective-permute-start | bytes 3145736 | tf_op jit(solution)/shard_map/cond/branch_1_fun/ppermute | solution.py:375
  81.0 4.2 %collective-permute-done.13.a_ref.refs_8_ = f32[256,512]{1,0:T(8,128)S(1)} collective-permute-done((f32[256,512]{1,0:T(8,128)S(1)}, f32[256,512]{1,0:T(8,128)S(1)}, u32[]{:S(2)}, u32[]{:S(2)}) %collective-permute-start.13) | collective-permute-done | bytes 524320 | tf_op jit(solution)/shard_map/cond/branch_1_fun/ppermute | solution.py:377
  85.2 3.0 %collective-permute-done.14.b_ref.refs_9_ = f32[256,512]{1,0:T(8,128)S(1)} collective-permute-done((f32[256,512]{1,0:T(8,128)S(1)}, f32[256,512]{1,0:T(8,128)S(1)}, u32[]{:S(2)}, u32[]{:S(2)}) %collective-permute-start.14) | collective-permute-done | bytes 524320 | tf_op jit(solution)/shard_map/cond/branch_1_fun/ppermute | solution.py:377
  88.8 1.3 %collective-permute-start.17 = (f32[256,512]{1,0:T(8,128)S(1)}, f32[256,512]{1,0:T(8,128)S(1)}, u32[]{:S(2)}, u32[]{:S(2)}) collective-permute-start(f32[256,512]{1,0:T(8,128)S(1)} %branch_1_fun.14), channel_id=1, source_target_pairs={{5,4},{3,2},{7,6},{1,0},{13,12},{11,10},{15,14},{9,8},{21,20},{19,... | collective-permute-start | bytes 1572872 | tf_op jit(solution)/shard_map/cond/branch_1_fun/ppermute | solution.py:386
  90.1 1.5 %collective-permute-done.17.refs_11_ = f32[256,512]{1,0:T(8,128)S(1)} collective-permute-done((f32[256,512]{1,0:T(8,128)S(1)}, f32[256,512]{1,0:T(8,128)S(1)}, u32[]{:S(2)}, u32[]{:S(2)}) %collective-permute-start.17) | collective-permute-done | bytes 524320 | tf_op jit(solution)/shard_map/cond/branch_1_fun/ppermute | solution.py:386
  91.6 1.5 %branch_1_fun.15 = f32[256,512]{1,0:T(8,128)S(1)} custom-call(s32[2]{0:T(128)S(1)} %get-tuple-element.56.place, s32[1,512]{1,0:T(1,128)S(1)} %copy-done.7, s32[8,512]{1,0:T(8,128)S(1)} %get-tuple-element.58.ranks_ref.refs_1_, f32[256,512]{1,0:T(8,128)S(1)} %copy-done.1, f32[256,512]{1,0:T(8,128)S(1)} %get-tuple-element.87.refs_3_, ...), custom_call_target="tpu_custom_call" | custom-call | tf_op jit(solution)/shard_map/cond/branch_1_fun/pallas_call | solution.py:356
  93.1 0.8 copy-done.6
  (28 shorter events, 2.4 us)
Async XLA Ops:
  0.0 11.2 %collective-permute-start.29 = (f32[256,512]{1,0:T(8,128)}, f32[256,512]{1,0:T(8,128)S(1)}, u32[]{:S(2)}, u32[]{:S(2)}) collective-permute-start(f32[256,512]{1,0:T(8,128)} %param.6), channel_id=1, source_target_pairs={{0,1},{1,0},{2,2},{3,3},{4,4},{5,5},{6,6},{7,7},{8,9},{9,8},{10,10... | collective-permute-start | bytes 1572872 | tf_op jit(solution)/shard_map/ppermute | solution.py:371
  11.4 51.8 %copy-start.7 = (s32[1,512]{1,0:T(1,128)S(1)}, s32[1,512]{1,0:T(1,128)}, u32[]{:S(2)}) copy-start(s32[1,512]{1,0:T(1,128)} %get-tuple-element.57.piv_ref.refs_0_) | copy-start | bytes 6148 | tf_op jit(solution)/shard_map/cond
  11.4 55.6 %copy-start.3 = (f32[4,128,128]{2,1,0:T(8,128)S(1)}, f32[4,128,128]{2,1,0:T(8,128)}, u32[]{:S(2)}) copy-start(f32[4,128,128]{2,1,0:T(8,128)} %get-tuple-element.76.linv) | copy-start | bytes 786436 | tf_op jit(solution)/shard_map/cond
  11.4 55.6 %copy-start.5 = (f32[4,128,128]{2,1,0:T(8,128)S(1)}, f32[4,128,128]{2,1,0:T(8,128)}, u32[]{:S(2)}) copy-start(f32[4,128,128]{2,1,0:T(8,128)} %get-tuple-element.77.uinv) | copy-start | bytes 786436 | tf_op jit(solution)/shard_map/cond
  13.2 29.4 %collective-permute-start = (f32[96,512]{1,0:T(8,128)S(1)}, f32[96,512]{1,0:T(8,128)S(1)}, u32[]{:S(2)}, u32[]{:S(2)}) collective-permute-start(f32[96,512]{1,0:T(8,128)S(1)} %get-tuple-element.63), channel_id=1, source_target_pairs={{0,128},{8,136},{1,129},{9,137},{2,130},{10,138},{3,131},{11,139},... | collective-permute-start | bytes 589832 | tf_op jit(solution)/shard_map/cond/branch_1_fun/ppermute | solution.py:408
  14.5 28.1 %collective-permute-start.1 = (f32[96,512]{1,0:T(8,128)S(1)}, f32[96,512]{1,0:T(8,128)S(1)}, u32[]{:S(2)}, u32[]{:S(2)}) collective-permute-start(f32[96,512]{1,0:T(8,128)S(1)} %get-tuple-element.64), channel_id=1, source_target_pairs={{0,384},{8,392},{1,385},{9,393},{2,386},{10,394},{3,387},{11,395},... | collective-permute-start | bytes 589832 | tf_op jit(solution)/shard_map/cond/branch_1_fun/ppermute | solution.py:408
  15.8 26.8 %collective-permute-start.2 = (f32[96,512]{1,0:T(8,128)S(1)}, f32[96,512]{1,0:T(8,128)S(1)}, u32[]{:S(2)}, u32[]{:S(2)}) collective-permute-start(f32[96,512]{1,0:T(8,128)S(1)} %get-tuple-element.65), channel_id=1, source_target_pairs={{0,256},{8,264},{1,257},{9,265},{2,258},{10,266},{3,259},{11,267},... | collective-permute-start | bytes 589832 | tf_op jit(solution)/shard_map/cond/branch_1_fun/ppermute | solution.py:408
  44.5 21.1 %collective-permute-start.10 = (f32[176,512]{1,0:T(8,128)S(1)}, f32[176,512]{1,0:T(8,128)S(1)}, u32[]{:S(2)}, u32[]{:S(2)}) collective-permute-start(f32[176,512]{1,0:T(8,128)S(1)} %get-tuple-element.75.a0), channel_id=1, source_target_pairs={{0,128},{8,136},{16,144},{24,152},{32,160},{40,168},{48,176},{56,1... | collective-permute-start | bytes 1081352 | tf_op jit(solution)/shard_map/cond/branch_1_fun/ppermute | solution.py:367
  47.9 19.1 %collective-permute-start.11 = (f32[176,512]{1,0:T(8,128)S(1)}, f32[176,512]{1,0:T(8,128)S(1)}, u32[]{:S(2)}, u32[]{:S(2)}) collective-permute-start(f32[176,512]{1,0:T(8,128)S(1)} %get-tuple-element.75.a0), channel_id=1, source_target_pairs={{0,256},{8,264},{16,272},{24,280},{32,288},{40,296},{48,304},{56,3... | collective-permute-start | bytes 1081352 | tf_op jit(solution)/shard_map/cond/branch_1_fun/ppermute | solution.py:367
  52.2 14.8 %collective-permute-start.12 = (f32[176,512]{1,0:T(8,128)S(1)}, f32[176,512]{1,0:T(8,128)S(1)}, u32[]{:S(2)}, u32[]{:S(2)}) collective-permute-start(f32[176,512]{1,0:T(8,128)S(1)} %get-tuple-element.75.a0), channel_id=1, source_target_pairs={{0,384},{8,392},{16,400},{24,408},{32,416},{40,424},{48,432},{56,4... | collective-permute-start | bytes 1081352 | tf_op jit(solution)/shard_map/cond/branch_1_fun/ppermute | solution.py:367
  55.3 3.2 %collective-permute-start.3 = (f32[40,512]{1,0:T(8,128)S(1)}, f32[40,512]{1,0:T(8,128)S(1)}, u32[]{:S(2)}, u32[]{:S(2)}) collective-permute-start(f32[40,512]{1,0:T(8,128)S(1)} %get-tuple-element.66), channel_id=1, source_target_pairs={{0,16},{8,24},{128,144},{136,152},{256,272},{264,280},{384,400},{3... | collective-permute-start | bytes 245768 | tf_op jit(solution)/shard_map/cond/branch_1_fun/ppermute | solution.py:416
  56.7 3.5 %collective-permute-start.4 = (f32[40,512]{1,0:T(8,128)S(1)}, f32[40,512]{1,0:T(8,128)S(1)}, u32[]{:S(2)}, u32[]{:S(2)}) collective-permute-start(f32[40,512]{1,0:T(8,128)S(1)} %get-tuple-element.67), channel_id=1, source_target_pairs={{0,112},{8,120},{128,240},{136,248},{256,368},{264,376},{384,496},... | collective-permute-start | bytes 245768 | tf_op jit(solution)/shard_map/cond/branch_1_fun/ppermute | solution.py:416
  58.5 3.2 %collective-permute-start.5 = (f32[40,512]{1,0:T(8,128)S(1)}, f32[40,512]{1,0:T(8,128)S(1)}, u32[]{:S(2)}, u32[]{:S(2)}) collective-permute-start(f32[40,512]{1,0:T(8,128)S(1)} %get-tuple-element.68), channel_id=1, source_target_pairs={{0,48},{8,56},{128,176},{136,184},{256,304},{264,312},{384,432},{3... | collective-permute-start | bytes 245768 | tf_op jit(solution)/shard_map/cond/branch_1_fun/ppermute | solution.py:416
  60.2 2.9 %collective-permute-start.6 = (f32[40,512]{1,0:T(8,128)S(1)}, f32[40,512]{1,0:T(8,128)S(1)}, u32[]{:S(2)}, u32[]{:S(2)}) collective-permute-start(f32[40,512]{1,0:T(8,128)S(1)} %get-tuple-element.69), channel_id=1, source_target_pairs={{0,80},{8,88},{128,208},{136,216},{256,336},{264,344},{384,464},{3... | collective-permute-start | bytes 245768 | tf_op jit(solution)/shard_map/cond/branch_1_fun/ppermute | solution.py:416
  63.7 8.4 %collective-permute-start.7 = (f32[16,512]{1,0:T(8,128)S(1)}, f32[16,512]{1,0:T(8,128)S(1)}, u32[]{:S(2)}, u32[]{:S(2)}) collective-permute-start(f32[16,512]{1,0:T(8,128)S(1)} %get-tuple-element.71), channel_id=1, source_target_pairs={{16,24},{48,56},{80,88},{112,120},{144,152},{176,184},{208,216},{2... | collective-permute-start | bytes 98312 | tf_op jit(solution)/shard_map/cond/branch_1_fun/ppermute | solution.py:423
  64.4 7.8 %collective-permute-start.8 = (f32[16,512]{1,0:T(8,128)S(1)}, f32[16,512]{1,0:T(8,128)S(1)}, u32[]{:S(2)}, u32[]{:S(2)}) collective-permute-start(f32[16,512]{1,0:T(8,128)S(1)} %get-tuple-element.72), channel_id=1, source_target_pairs={{16,0},{48,32},{80,64},{112,96},{144,128},{176,160},{208,192},{240... | collective-permute-start | bytes 98312 | tf_op jit(solution)/shard_map/cond/branch_1_fun/ppermute | solution.py:423
  65.7 6.8 %collective-permute-start.9 = (f32[16,512]{1,0:T(8,128)S(1)}, f32[16,512]{1,0:T(8,128)S(1)}, u32[]{:S(2)}, u32[]{:S(2)}) collective-permute-start(f32[16,512]{1,0:T(8,128)S(1)} %get-tuple-element.73), channel_id=1, source_target_pairs={{16,8},{48,40},{80,72},{112,104},{144,136},{176,168},{208,200},{24... | collective-permute-start | bytes 98312 | tf_op jit(solution)/shard_map/cond/branch_1_fun/ppermute | solution.py:423
  72.1 8.3 %copy-start.1 = (f32[256,512]{1,0:T(8,128)S(1)}, f32[256,512]{1,0:T(8,128)}, u32[]{:S(2)}) copy-start(f32[256,512]{1,0:T(8,128)} %get-tuple-element.59.refs_2_) | copy-start | bytes 1572868 | tf_op jit(solution)/shard_map/cond
  73.1 12.1 %collective-permute-start.13 = (f32[256,512]{1,0:T(8,128)S(1)}, f32[256,512]{1,0:T(8,128)S(1)}, u32[]{:S(2)}, u32[]{:S(2)}) collective-permute-start(f32[256,512]{1,0:T(8,128)S(1)} %get-tuple-element.81.refs_7_), channel_id=1, source_target_pairs={{1,5},{0,1},{9,13},{8,9},{17,21},{16,17},{25,29},{24,25},{33,37},{... | collective-permute-start | bytes 1572872 | tf_op jit(solution)/shard_map/cond/branch_1_fun/ppermute | solution.py:377
  76.5 11.7 %collective-permute-start.14 = (f32[256,512]{1,0:T(8,128)S(1)}, f32[256,512]{1,0:T(8,128)S(1)}, u32[]{:S(2)}, u32[]{:S(2)}) collective-permute-start(f32[256,512]{1,0:T(8,128)S(1)} %get-tuple-element.81.refs_7_), channel_id=1, source_target_pairs={{1,3},{9,11},{17,19},{25,27},{33,35},{41,43},{49,51},{57,59},{65,6... | collective-permute-start | bytes 1572872 | tf_op jit(solution)/shard_map/cond/branch_1_fun/ppermute | solution.py:377
  77.8 10.4 %collective-permute-start.15 = (f32[256,512]{1,0:T(8,128)S(1)}, f32[256,512]{1,0:T(8,128)S(1)}, u32[]{:S(2)}, u32[]{:S(2)}) collective-permute-start(f32[256,512]{1,0:T(8,128)S(1)} %get-tuple-element.81.refs_7_), channel_id=1, source_target_pairs={{1,7},{9,15},{17,23},{25,31},{33,39},{41,47},{49,55},{57,63},{65,7... | collective-permute-start | bytes 1572872 | tf_op jit(solution)/shard_map/cond/branch_1_fun/ppermute | solution.py:377
  79.1 11.0 %collective-permute-start.16 = (f32[512,512]{1,0:T(8,128)S(1)}, f32[512,512]{1,0:T(8,128)S(1)}, u32[]{:S(2)}, u32[]{:S(2)}) collective-permute-start(f32[512,512]{1,0:T(8,128)S(1)} %get-tuple-element.83.refs_4_), channel_id=1, source_target_pairs={{0,1},{8,9},{16,17},{24,25},{32,33},{40,41},{48,49},{56,57},{64,65... | collective-permute-start | bytes 3145736 | tf_op jit(solution)/shard_map/cond/branch_1_fun/ppermute | solution.py:375
  88.8 2.8 %collective-permute-start.17 = (f32[256,512]{1,0:T(8,128)S(1)}, f32[256,512]{1,0:T(8,128)S(1)}, u32[]{:S(2)}, u32[]{:S(2)}) collective-permute-start(f32[256,512]{1,0:T(8,128)S(1)} %branch_1_fun.14), channel_id=1, source_target_pairs={{5,4},{3,2},{7,6},{1,0},{13,12},{11,10},{15,14},{9,8},{21,20},{19,... | collective-permute-start | bytes 1572872 | tf_op jit(solution)/shard_map/cond/branch_1_fun/ppermute | solution.py:386
  93.1 0.8 copy-start.6
